TPU v7x, 128 devices: a whole 4x4x4 slice. The times are simulated.
128 devices in a mesh: gx: 8 (over z_lo, x), gy: 16 (over z_hi, y, core).
Axes of the slice: x: 4, y: 4, z: 4 (z_hi: 2, z_lo: 2; z = z_hi * 2 + z_lo), core: 2. Of those that a mesh axis runs over, the one named last changes fastest.
Arguments:
- velocity: float32 [3, 256, 1024, 128], P(None, 'gx', 'gy'), may hold values from -6 to 6
- stress: float32 [6, 256, 1024, 128], P(None, 'gx', 'gy'), may hold values from -6 to 6
- region_id: int32 [256, 1024, 128], P('gx', 'gy'), may hold values from 0 to 15
- buoyancy: float32 [16], replicated, may hold values from 0.5 to 1
- lame_lambda: float32 [16], replicated, may hold values from 0.5 to 2
- shear_mu: float32 [16], replicated, may hold values from 0.25 to 1
- shell_rows: float32 [32768, 9, 128], P(('gx', 'gy')), may hold values from -6 to 6
- shell_target: int32 [32768, 1], P(('gx', 'gy')), may hold values from 0 to 127; in each aligned block of 256 rows (0 to 255, 256 to 511, ...) at most 4 rows name the same one
- shell_cell: int32 [32768, 1], P(('gx', 'gy')), may hold values from 0 to 2047
- pile_pier: int32 [32768, 1], P(('gx', 'gy')), may hold values from 0 to 127; in each aligned block of 256 rows (0 to 255, 256 to 511, ...) at most 4 rows name the same one
- pile_cell: int32 [32768, 1], P(('gx', 'gy')), may hold values from 0 to 2047
- pier_owner: int32 [128], replicated, may hold values from 0 to 127, each once
Outputs:
- velocity_out: float32 [3, 256, 1024, 128], P(None, 'gx', 'gy')
- stress_out: float32 [6, 256, 1024, 128], P(None, 'gx', 'gy')
- pier_force: float32 [128, 384], P(('gx', 'gy'))
Inputs may be any that keep to these rules, and one draw needn't show every extreme that they name: `shell_target`: within the rows of one device (aligned blocks of 256 rows), no device number appears more than 4 times, and some number appears exactly 4 times. `shell_cell`: A column number inside the target device's block. `pile_pier`: within the rows of one device (aligned blocks of 256 rows), no pier appears more than 4 times, and some pier appears exactly 4 times. `pile_cell`: A column number inside the block of the device that lists the pile. `pier_owner`: A permutation; the pier with owner slot s is owned by device s.
All inputs are finite; a program needn't handle non-finite values.
Results may differ from a plain program's by a relative error of at most 0.00002.
Values sent between devices are 32-bit elements; how exact they have to be, the bound alone decides.
A program may use at most 192 MiB of HBM per device.

v0:
```python
import jax
import jax.numpy as jnp
from jax import lax
from jax.sharding import PartitionSpec as P

PML = 8


STEP = 0.25
DAMP = 0.3


def with_halo(x, sides, width):
    for axis, dim in sides:
        devices, length = (lax.axis_size(axis), x.shape[dim])
        up = [(i, (i + 1) % devices) for i in range(devices - 1)]
        down = [(j, i) for i, j in up]
        last = lax.slice_in_dim(x, length - width, length, axis=dim)
        leading = lax.slice_in_dim(x, 0, width, axis=dim)
        before = lax.ppermute(last, axis, up)
        after = lax.ppermute(leading, axis, down)
        x = jnp.concatenate([before, x, after], axis=dim)
    return x


def absorb(distance):
    ramp = jnp.maximum(0.0, (PML - distance) / PML)
    return 1.0 - DAMP * ramp * ramp


def damping(x_index, x_total, y_index, y_total, depth):
    along_x = absorb(jnp.minimum(x_index, x_total - 1 - x_index).astype(jnp.float32))
    along_y = absorb(jnp.minimum(y_index, y_total - 1 - y_index).astype(jnp.float32))
    depth_index = jnp.arange(depth, dtype=jnp.int32)
    along_z = absorb((depth - 1 - depth_index).astype(jnp.float32))
    return along_x[:, None, None] * along_y[None, :, None] * along_z[None, None, :]


def shift_up(values):
    return jnp.concatenate([values[..., 1:], jnp.zeros_like(values[..., :1])], axis=-1) - values


def shift_down(values):
    return values - jnp.concatenate([jnp.zeros_like(values[..., :1]), values[..., :-1]], axis=-1)


def differences(padded):
    middle = padded[:, 1:-1, 1:-1]

    def ahead_x(field):
        return padded[field, 2:, 1:-1] - middle[field]

    def behind_x(field):
        return middle[field] - padded[field, :-2, 1:-1]

    def ahead_y(field):
        return padded[field, 1:-1, 2:] - middle[field]

    def behind_y(field):
        return middle[field] - padded[field, 1:-1, :-2]

    return (middle, ahead_x, behind_x, ahead_y, behind_y)


def move_velocity(velocity, padded, buoyant):
    middle, ahead_x, behind_x, ahead_y, behind_y = differences(padded)
    scaled = STEP * buoyant
    velocity_x = velocity[0] + scaled * (ahead_x(0) + behind_y(3) + shift_down(middle[4]))
    velocity_y = velocity[1] + scaled * (behind_x(3) + ahead_y(1) + shift_down(middle[5]))
    velocity_z = velocity[2] + scaled * (behind_x(4) + behind_y(5) + shift_up(middle[2]))
    return jnp.stack([velocity_x, velocity_y, velocity_z])


def move_stress(stress, padded, lame_first, shear_cells):
    middle, ahead_x, behind_x, ahead_y, behind_y = differences(padded)
    strain_xx = behind_x(0)
    strain_yy = behind_y(1)
    strain_zz = shift_down(middle[2])
    dilation = strain_xx + strain_yy + strain_zz
    stress_xx = stress[0] + STEP * (lame_first * dilation + 2.0 * shear_cells * strain_xx)
    stress_yy = stress[1] + STEP * (lame_first * dilation + 2.0 * shear_cells * strain_yy)
    stress_zz = stress[2] + STEP * (lame_first * dilation + 2.0 * shear_cells * strain_zz)
    stress_xy = stress[3] + STEP * shear_cells * (ahead_x(1) + ahead_y(0))
    stress_xz = stress[4] + STEP * shear_cells * (ahead_x(2) + shift_up(middle[0]))
    stress_yz = stress[5] + STEP * shear_cells * (ahead_y(2) + shift_up(middle[1]))
    return jnp.stack([stress_xx, stress_yy, stress_zz, stress_xy, stress_xz, stress_yz])


def lookup(region_id, table):
    result = jnp.zeros(region_id.shape, jnp.float32)
    for region in range(table.shape[0]):
        result = jnp.where(region_id == region, table[region], result)
    return result


def rank_within(labels):
    positions = jnp.arange(labels.shape[0], dtype=jnp.int32)
    earlier = (labels[:, None] == labels[None, :]) & (positions[None, :] < positions[:, None])
    return jnp.sum(earlier.astype(jnp.int32), axis=1)


def on_device(
    velocity,
    stress,
    region_id,
    buoyancy,
    lame_lambda,
    shear_mu,
    shell_rows,
    shell_target,
    shell_cell,
    pile_pier,
    pile_cell,
    pier_owner,
):
    count_x = lax.axis_size("gx")
    count_y = lax.axis_size("gy")
    devices = count_x * count_y
    width_x = velocity.shape[1]
    width_y = velocity.shape[2]
    depth = velocity.shape[3]
    cells = width_x * width_y
    shell_dev = shell_rows.shape[0]
    capacity = max(2, (2 * shell_dev + devices - 1) // devices)
    target = shell_target[:, 0]
    send_slot = target * capacity + rank_within(target)
    outgoing = jnp.zeros((devices * capacity, 9, depth), jnp.float32).at[send_slot].set(shell_rows)
    out_cells = (
        jnp.zeros((devices * capacity,), jnp.float32)
        .at[send_slot]
        .set(shell_cell[:, 0].astype(jnp.float32))
    )
    arrived, arrived_cells = (
        lax.all_to_all(outgoing, ("gx", "gy"), split_axis=0, concat_axis=0, tiled=True),
        lax.all_to_all(out_cells, ("gx", "gy"), split_axis=0, concat_axis=0, tiled=True),
    )
    into_cells = arrived_cells.astype(jnp.int32)
    moved = jnp.transpose(arrived, (1, 0, 2))
    velocity_in = (
        velocity.reshape(3, cells, depth).at[:, into_cells].add(moved[:3]).reshape(velocity.shape)
    )
    stress_in = (
        stress.reshape(6, cells, depth).at[:, into_cells].add(moved[3:]).reshape(stress.shape)
    )
    buoyant = lookup(region_id, buoyancy)
    lame_first = lookup(region_id, lame_lambda)
    shear_cells = lookup(region_id, shear_mu)
    stress_pad = with_halo(stress_in, (("gx", 1), ("gy", 2)), 1)
    velocity_new = move_velocity(velocity_in, stress_pad, buoyant)
    velocity_pad = with_halo(velocity_new, (("gx", 1), ("gy", 2)), 1)
    stress_new = move_stress(stress_in, velocity_pad, lame_first, shear_cells)
    x_index = lax.axis_index("gx") * width_x + jnp.arange(width_x, dtype=jnp.int32)
    y_index = lax.axis_index("gy") * width_y + jnp.arange(width_y, dtype=jnp.int32)
    factor = damping(x_index, width_x * count_x, y_index, width_y * count_y, depth)
    velocity_out = velocity_new * factor
    stress_out = stress_new * factor
    piers = pier_owner.shape[0]
    pile_dev = pile_cell.shape[0]
    pier_dev = piers // devices
    pier_cap = max(2, (2 * pile_dev + piers - 1) // piers)
    traction = jnp.stack([stress_out[4], stress_out[5], stress_out[2]]).reshape(3, cells, depth)[
        :, pile_cell[:, 0]
    ]
    traction = jnp.transpose(traction, (1, 0, 2))
    pier_label = pile_pier[:, 0]
    pier_ids = jnp.arange(piers, dtype=jnp.int32)
    owner_slot = jnp.sum(
        jnp.where(pier_label[:, None] == pier_ids[None, :], pier_owner[None, :], 0), axis=1
    )
    row_slot = owner_slot * pier_cap + rank_within(pier_label)
    outgoing_rows = jnp.zeros((piers * pier_cap, 3, depth), jnp.float32).at[row_slot].set(traction)
    received = lax.all_to_all(outgoing_rows, ("gx", "gy"), split_axis=0, concat_axis=0, tiled=True)
    summed = jnp.sum(jnp.tanh(received).reshape(devices, pier_dev, pier_cap, 3, depth), axis=(0, 2))
    pier_force = (summed * (pier_dev / pile_dev) ** 0.5).reshape(pier_dev, 3 * depth)
    return (velocity_out, stress_out, pier_force)


def solution(mesh):
    return jax.shard_map(
        on_device,
        mesh=mesh,
        in_specs=(
            P(None, "gx", "gy", None),
            P(None, "gx", "gy", None),
            P("gx", "gy", None),
            P(),
            P(),
            P(),
            P(("gx", "gy"), None, None),
            P(("gx", "gy"), None),
            P(("gx", "gy"), None),
            P(("gx", "gy"), None),
            P(("gx", "gy"), None),
            P(),
        ),
        out_specs=(P(None, "gx", "gy", None), P(None, "gx", "gy", None), P(("gx", "gy"), None)),
        check_vma=False,
    )
```

profile of v0, /device:TPU:1, one launch (start us, length us, event | category | flops | bytes accessed | tf_op | source)
XLA Modules:
  0.0 424.1 jit_solution(6980799655722404721)
XLA Ops:
  0.6 0.9 convert_reduce_fusion.1
  1.6 0.7 compare_select_fusion.3
  2.3 0.7 convert_element_type.47
  2.9 1.4 scatter_custom_fusion
  4.3 0.7 all_to_all.12
  5.1 11.5 %all-to-all-start = ((f32[128,4,1]{1,2,0:T(1,128)}), f32[128,4,1]{1,2,0:T(1,128)S(1)}, u32[]{:S(2)}, u32[]{:S(2)}) async-start(f32[128,4,1]{1,2,0:T(1,128)} %bitcast.5), calls=%async_computation | async-start | bytes 131072 | tf_op jit(solution)/shard_map/all_to_all | solution.py:135
  16.6 2.0 copy.43
  18.6 2.3 broadcast_in_dim.184
  20.9 26.5 %scatter_fusion = f32[512,9,128]{2,1,0:T(8,128)} fusion(f32[512,9,128]{2,1,0:T(8,128)} %broadcast_in_dim.184, s32[256]{0:T(256)S(1)} %bitcast.274, f32[256,9,128]{2,1,0:T(8,128)S(1)} %copy.43), kind=kCustom, calls=%fused_computation.2 | custom fusion | bytes 3539968 | tf_op jit(solution)/shard_map/scatter | solution.py:127
  47.4 10.8 %all-to-all-start.1 = ((f32[512,9,128]{2,1,0:T(8,128)}), f32[512,9,128]{2,1,0:T(8,128)}, u32[]{:S(2)}, u32[]{:S(2)}) async-start(f32[512,9,128]{2,1,0:T(8,128)} %scatter_fusion), calls=%async_computation.1 | async-start | bytes 8388608 | tf_op jit(solution)/shard_map/all_to_all | solution.py:134
  58.2 11.8 %copy.44 = f32[6,32,64,128]{3,0,2,1:T(8,128)} copy(f32[6,32,64,128]{3,2,1,0:T(8,128)} %param.13) | data formatting | bytes 12582912 | tf_op args[1]
  70.1 4.5 %copy.41 = f32[3,32,64,128]{3,0,2,1:T(4,128)} copy(f32[3,32,64,128]{3,2,1,0:T(8,128)S(1)} %copy-done.9) | data formatting | bytes 6291456 | tf_op args[0]
  74.7 0.7 fusion.69
  75.4 0.7 fusion.67
  76.1 0.2 select_reduce_fusion
  76.3 0.2 convert_reduce_fusion
  76.6 1.3 broadcast_multiply_fusion.2
  77.9 0.2 convert_reduce_fusion.2
  78.3 36.2 %all-to-all-done.1 = f32[512,9,128]{2,1,0:T(8,128)} async-done(((f32[512,9,128]{2,1,0:T(8,128)}), f32[512,9,128]{2,1,0:T(8,128)}, u32[]{:S(2)}, u32[]{:S(2)}) %all-to-all-start.1) | async-done | bytes 2359328 | tf_op jit(solution)/shard_map/all_to_all | solution.py:134
  114.5 2.4 slice_bitcast_fusion
  116.9 56.7 %scatter_fusion.2 = f32[6,2048,128]{2,0,1:T(8,128)} fusion(f32[6,2048,128]{2,0,1:T(8,128)} %bitcast.225, s32[512]{0:T(512)S(1)} %bitcast.264, f32[512,6,128]{2,1,0:T(8,128)S(1)} %slice_bitcast_fusion), kind=kCustom, calls=%fused_computation.4 | custom fusion | flops 393216 | bytes 4720640 | tf_op jit(solution)/shard_map/scatter-add | solution.py:143
  173.6 34.6 %fusion.62 = (f32[1,2048,128]{2,0,1:T(1,128)}, f32[1,2048,128]{2,0,1:T(1,128)}, f32[1,2048,128]{2,0,1:T(1,128)}, f32[1,2048,128]{2,0,1:T(1,128)S(1)}, f32[1,2048,128]{2,0,1:T(1,128)}, /*index=5*/f32[1,2048,128]{2,0,1:T(1,128)}) fusion(f32[6,2048,128]{2,0,1:T(8,128)} %scatter_fusion.2), kind=kLoop, calls=%fused_computation.152 | loop fusion | bytes 12582912 | tf_op jit(solution)/shard_map/slice | solution.py:57
  208.1 4.6 %copy.46 = f32[6,32,64,128]{3,2,1,0:T(8,128)S(1)} copy(f32[6,32,64,128]{3,0,2,1:T(8,128)} %bitcast.226) | data formatting | bytes 12582912 | tf_op jit(solution)/shard_map/reshape | solution.py:143
  212.8 2.7 copy-done
  215.5 1.3 collective-permute-start.1
  216.8 1.3 collective-permute-start
  218.1 1.7 slice_bitcast_fusion.3
  219.9 54.0 %scatter_fusion.1 = f32[3,2048,128]{2,0,1:T(4,128)} fusion(f32[3,2048,128]{2,0,1:T(4,128)} %bitcast.255, s32[512]{0:T(512)S(1)} %bitcast.265, f32[512,3,128]{2,1,0:T(4,128)S(1)} %slice_bitcast_fusion.3), kind=kCustom, calls=%fused_computation.3 | custom fusion | flops 196608 | bytes 2361344 | tf_op jit(solution)/shard_map/scatter-add | solution.py:140
  273.8 0.8 constant_dynamic-update-slice_fusion.4
  274.6 7.6 %constant_dynamic-update-slice_fusion.3 = (f32[6,33,64,128]{3,2,1,0:T(8,128)}, f32[6,34,64,128]{3,2,1,0:T(8,128)S(1)}) fusion(f32[6,33,64,128]{3,2,1,0:T(8,128)} %get-tuple-element.48, f32[6,34,64,128]{3,2,1,0:T(8,128)S(1)} %get-tuple-element.49, f32[6,32,64,128]{3,0,2,1:T(8,128)} %bitcast.227), kind=kLoop, calls=%fused_computation.123 | loop fusion | bytes 20971520 | tf_op jit(solution)/shard_map/concatenate | solution.py:22
  282.2 0.1 fusion.63
  282.4 2.2 collective-permute-start.2
  284.6 8.5 %fusion.65 = (f32[1,2048,128]{2,0,1:T(1,128)}, f32[1,2048,128]{2,0,1:T(1,128)}, f32[1,2048,128]{2,0,1:T(1,128)S(1)}) fusion(f32[3,2048,128]{2,0,1:T(4,128)} %scatter_fusion.1), kind=kLoop, calls=%fused_computation.155 | loop fusion | bytes 6291456 | tf_op jit(solution)/shard_map/slice | solution.py:69
  293.1 1.3 slice.401
  294.4 10.8 %collective-permute-start.3 = (f32[6,34,1,128]{3,2,1,0:T(1,128)S(1)}, f32[6,34,1,128]{3,2,1,0:T(1,128)S(1)}, u32[]{:S(2)}, u32[]{:S(2)}) collective-permute-start(f32[6,34,1,128]{3,2,1,0:T(1,128)S(1)} %get-tuple-element.33), channel_id=1, source_target_pairs={{1,0},{2,1},{3,2},{4,3},{5,4},{6,5},{7,6},{8,7},{9,8},{10,9},{11,1... | collective-permute-start | bytes 313352 | tf_op jit(solution)/shard_map/ppermute | solution.py:21
  305.4 16.7 %fusion.43 = (f32[32,64,128]{2,1,0:T(8,128)S(1)}, f32[32,64,128]{2,1,0:T(8,128)}, pred[32,64,128]{2,1,0:T(8,128)(4,1)S(1)}, pred[32,64,128]{2,1,0:T(8,128)(4,1)S...) fusion(f32[32,64,128]{2,1,0:T(8,128)S(1)} %bitcast.263, ...), kind=kLoop, calls=%fused_computation.77 | loop fusion | flops 11010048 | bytes 25851968 | tf_op jit(solution)/shard_map/add | solution.py:68
  322.1 4.7 %fusion.37 = (f32[32,64,128]{2,1,0:T(8,128)S(1)}, f32[32,64,128]{2,1,0:T(8,128)S(1)}) fusion(f32[32,64,128]{2,1,0:T(8,128)} %bitcast.261, f32[32,64,128]{2,1,0:T(8,128)} %get-tuple-element.8, f32[32,64,128]{2,1,0:T(8,128)S(1)} %bitcast.256, f32[6,34,1,128]{3,2,1,0:T(1,128)S(1)} %collective-permute-done.3, ...), kind=kLoop, calls=%fused_computation.69 | loop fusion | flops 4194304 | bytes 21557248 | tf_op jit(solution)/shard_map/add | solution.py:69
  326.8 2.5 pad_maximum_fusion
  329.5 1.6 collective-permute-start.4
  331.1 1.3 collective-permute-start.5
  332.4 0.7 fusion.68
  333.1 0.1 collective-permute-done.4
  333.2 4.2 collective-permute-done.5
  337.5 1.9 collective-permute-start.6
  339.5 0.3 slice.405
  339.8 0.3 slice.406
  340.2 2.4 collective-permute-start.7
  342.7 24.0 %bitcast_dynamic-update-slice_fusion.2 = (f32[6,32,64,128]{3,2,1,0:T(8,128)S(1)}, f32[32,64,128]{2,1,0:T(8,128)S(1)}, f32[32,64,128]{2,1,0:T(8,128)S(1)}, f32[32,64,128]{2,1,0:T(8,128)S(1)}) fusion(f32[32,64,128]{2,1,0:T(8,128)S(1)} %bitcast.259, pred[32,64,128]{2,1,0:T(8,128)(4,1)S(1)} %copy-done.23, pred[32,64,128]{2,1,0:T(8,128)(4,1)S(1)} %copy-done.22, ...), kind=kLoop, calls=%fused_computation.84 | loop fusion | flops 13369343 | bytes 17017984
  366.7 0.5 bitcast_dynamic-update-slice_fusion.1
  367.2 0.5 bitcast_dynamic-update-slice_fusion
  367.7 0.7 fusion.19
  368.4 0.7 fusion.13
  369.1 0.8 fusion.6
  369.9 0.8 broadcast_multiply_fusion
  370.8 0.1 slice.407
  371.0 0.4 pad_maximum_fusion.1
  371.4 2.1 copy-done.4
  373.5 4.5 %copy.50 = f32[3,32,64,128]{3,0,2,1:T(4,128)} copy(f32[3,32,64,128]{3,2,1,0:T(8,128)S(1)} %pad_maximum_fusion.1) | data formatting | bytes 6291456 | tf_op jit(solution)/shard_map/stack | solution.py:161
  378.0 3.2 gather_fusion
  381.2 0.1 broadcast_in_dim.233
  381.4 7.0 %scatter_fusion.3 = f32[512,3,128]{2,1,0:T(4,128)S(1)} fusion(f32[512,3,128]{2,1,0:T(4,128)S(1)} %broadcast_in_dim.233, s32[256]{0:T(256)S(1)} %bitcast.272, f32[256,3,128]{2,1,0:T(4,128)S(1)} %gather_fusion), kind=kCustom, calls=%fused_computation.5 | custom fusion | bytes 1180672 | tf_op jit(solution)/shard_map/scatter | solution.py:171
  388.3 34.4 %all_to_all.19 = f32[512,3,128]{2,1,0:T(4,128)S(1)} all-to-all(f32[512,3,128]{2,1,0:T(4,128)S(1)} %scatter_fusion.3), channel_id=1, replica_groups=mesh['gx'=8,'gy'=16] {'gx','gy'}, dimensions={0} | all-to-all | bytes 1572864 | tf_op jit(solution)/shard_map/all_to_all | solution.py:172
  422.7 0.6 tanh_reduce_fusion
  423.3 0.6 copy.54
  (90 shorter events, 0.6 us)
Async XLA Ops:
  5.1 42.3 %all-to-all-start = ((f32[128,4,1]{1,2,0:T(1,128)}), f32[128,4,1]{1,2,0:T(1,128)S(1)}, u32[]{:S(2)}, u32[]{:S(2)}) async-start(f32[128,4,1]{1,2,0:T(1,128)} %bitcast.5), calls=%async_computation | async-start | bytes 131072 | tf_op jit(solution)/shard_map/all_to_all | solution.py:135
  47.4 67.1 %all-to-all-start.1 = ((f32[512,9,128]{2,1,0:T(8,128)}), f32[512,9,128]{2,1,0:T(8,128)}, u32[]{:S(2)}, u32[]{:S(2)}) async-start(f32[512,9,128]{2,1,0:T(8,128)} %scatter_fusion), calls=%async_computation.1 | async-start | bytes 8388608 | tf_op jit(solution)/shard_map/all_to_all | solution.py:134
  58.2 11.8 %copy-start.9 = (f32[3,32,64,128]{3,2,1,0:T(8,128)S(1)}, f32[3,32,64,128]{3,2,1,0:T(8,128)}, u32[]{:S(2)}) copy-start(f32[3,32,64,128]{3,2,1,0:T(8,128)} %param.12) | copy-start | bytes 9437188
  70.0 4.6 %copy-start.26 = (f32[16]{0:T(128)S(1)}, f32[16]{0:T(128)}, u32[]{:S(2)}) copy-start(f32[16]{0:T(128)} %param.15) | copy-start | bytes 196
  70.0 5.4 %copy-start.27 = (f32[16]{0:T(128)S(1)}, f32[16]{0:T(128)}, u32[]{:S(2)}) copy-start(f32[16]{0:T(128)} %param.16) | copy-start | bytes 196
  70.0 6.1 %copy-start.29 = (s32[256,1]{0,1:T(1,128)S(1)}, s32[256,1]{0,1:T(1,128)}, u32[]{:S(2)}) copy-start(s32[256,1]{0,1:T(1,128)} %param.21) | copy-start | bytes 3076
  70.1 6.1 %copy-start.31 = (s32[128]{0:T(128)S(1)}, s32[128]{0:T(128)}, u32[]{:S(2)}) copy-start(s32[128]{0:T(128)} %param.23) | copy-start | bytes 1540
  70.1 6.4 %copy-start.30 = (s32[256,1]{0,1:T(1,128)S(1)}, s32[256,1]{0,1:T(1,128)}, u32[]{:S(2)}) copy-start(s32[256,1]{0,1:T(1,128)} %param.22) | copy-start | bytes 3076
  212.7 2.7 copy-start
  215.5 58.4 %collective-permute-start.1 = (f32[6,1,64,128]{3,2,1,0:T(8,128)S(1)}, f32[6,1,64,128]{3,2,1,0:T(8,128)S(1)}, u32[]{:S(2)}, u32[]{:S(2)}) collective-permute-start(f32[6,1,64,128]{3,2,1,0:T(8,128)S(1)} %get-tuple-element.38), channel_id=1, source_target_pairs={{0,16},{16,32},{32,48},{48,64},{64,80},{80,96},{96,112},{1,17},{17... | collective-permute-start | bytes 589832 | tf_op jit(solution)/shard_map/ppermute | solution.py:20
  216.8 65.4 %collective-permute-start = (f32[6,1,64,128]{3,2,1,0:T(8,128)S(1)}, f32[6,1,64,128]{3,2,1,0:T(8,128)S(1)}, u32[]{:S(2)}, u32[]{:S(2)}) collective-permute-start(f32[6,1,64,128]{3,2,1,0:T(8,128)S(1)} %get-tuple-element.37), channel_id=1, source_target_pairs={{16,0},{32,16},{48,32},{64,48},{80,64},{96,80},{112,96},{17,1},{33... | collective-permute-start | bytes 589832 | tf_op jit(solution)/shard_map/ppermute | solution.py:21
  274.6 30.7 %slice-start = ((s8[6291456]{0:T(1024)(128)(4,1)}), s8[4194304]{0:T(1024)(128)(4,1)S(1)}, s32[]{:S(2)}) async-start(s8[6291456]{0:T(1024)(128)(4,1)} %bitcast.240), calls=%async_computation.3 | async-start | bytes 8388608
  274.6 30.7 %slice-start.1 = ((s8[6291456]{0:T(1024)(128)(4,1)}), s8[2097152]{0:T(1024)(128)(4,1)S(1)}, s32[]{:S(2)}) async-start(s8[6291456]{0:T(1024)(128)(4,1)} %bitcast.240), calls=%async_computation.4 | async-start | bytes 4194304
  282.2 10.9 %copy-start.1 = (f32[1,2048,128]{2,0,1:T(1,128)S(1)}, f32[1,2048,128]{2,0,1:T(1,128)}, u32[]{:S(2)}) copy-start(f32[1,2048,128]{2,0,1:T(1,128)} %get-tuple-element.28) | copy-start | bytes 3145732
  282.2 23.1 %copy-start.3 = (f32[1,2048,128]{2,0,1:T(1,128)S(1)}, f32[1,2048,128]{2,0,1:T(1,128)}, u32[]{:S(2)}) copy-start(f32[1,2048,128]{2,0,1:T(1,128)} %get-tuple-element.31) | copy-start | bytes 3145732
  282.2 23.1 %copy-start.7 = (f32[1,2048,128]{2,0,1:T(1,128)S(1)}, f32[1,2048,128]{2,0,1:T(1,128)}, u32[]{:S(2)}) copy-start(f32[1,2048,128]{2,0,1:T(1,128)} %get-tuple-element.32) | copy-start | bytes 3145732
  282.2 23.1 %copy-start.24 = (s32[32,64,128]{2,1,0:T(8,128)S(1)}, s32[32,64,128]{2,1,0:T(8,128)}, u32[]{:S(2)}) copy-start(s32[32,64,128]{2,1,0:T(8,128)} %param.14) | copy-start | bytes 3145732
  282.2 23.1 %copy-start.25 = (f32[6,1,64,128]{3,2,1,0:T(8,128)}, f32[6,1,64,128]{3,2,1,0:T(8,128)S(1)}, u32[]{:S(2)}) copy-start(f32[6,1,64,128]{3,2,1,0:T(8,128)S(1)} %collective-permute-done) | copy-start | bytes 589828
  282.4 22.9 %collective-permute-start.2 = (f32[6,34,1,128]{3,2,1,0:T(1,128)S(1)}, f32[6,34,1,128]{3,2,1,0:T(1,128)S(1)}, u32[]{:S(2)}, u32[]{:S(2)}) collective-permute-start(f32[6,34,1,128]{3,2,1,0:T(1,128)S(1)} %get-tuple-element.34), channel_id=1, source_target_pairs={{0,1},{1,2},{2,3},{3,4},{4,5},{5,6},{6,7},{7,8},{8,9},{9,10},{10,1... | collective-permute-start | bytes 313352 | tf_op jit(solution)/shard_map/ppermute | solution.py:20
  294.4 27.6 %collective-permute-start.3 = (f32[6,34,1,128]{3,2,1,0:T(1,128)S(1)}, f32[6,34,1,128]{3,2,1,0:T(1,128)S(1)}, u32[]{:S(2)}, u32[]{:S(2)}) collective-permute-start(f32[6,34,1,128]{3,2,1,0:T(1,128)S(1)} %get-tuple-element.33), channel_id=1, source_target_pairs={{1,0},{2,1},{3,2},{4,3},{5,4},{6,5},{7,6},{8,7},{9,8},{10,9},{11,1... | collective-permute-start | bytes 313352 | tf_op jit(solution)/shard_map/ppermute | solution.py:21
  305.3 16.7 %copy-start.2 = (f32[1,2048,128]{2,0,1:T(1,128)S(1)}, f32[1,2048,128]{2,0,1:T(1,128)}, u32[]{:S(2)}) copy-start(f32[1,2048,128]{2,0,1:T(1,128)} %get-tuple-element.29) | copy-start | bytes 3145732
  305.3 16.7 %copy-start.5 = (f32[1,2048,128]{2,0,1:T(1,128)S(1)}, f32[1,2048,128]{2,0,1:T(1,128)}, u32[]{:S(2)}) copy-start(f32[1,2048,128]{2,0,1:T(1,128)} %get-tuple-element.27) | copy-start | bytes 3145732
  322.1 4.7 %copy-start.6 = (f32[32,64,128]{2,1,0:T(8,128)S(1)}, f32[32,64,128]{2,1,0:T(8,128)}, u32[]{:S(2)}) copy-start(f32[32,64,128]{2,1,0:T(8,128)} %broadcast_multiply_fusion.2) | copy-start | bytes 3145732
  326.8 5.6 %copy-start.28 = (f32[16]{0:T(128)S(1)}, f32[16]{0:T(128)}, u32[]{:S(2)}) copy-start(f32[16]{0:T(128)} %param.17) | copy-start | bytes 196
  329.4 13.2 %copy-start.8 = (f32[1,2048,128]{2,0,1:T(1,128)S(1)}, f32[1,2048,128]{2,0,1:T(1,128)}, u32[]{:S(2)}) copy-start(f32[1,2048,128]{2,0,1:T(1,128)} %get-tuple-element.32) | copy-start | bytes 3145732
  329.4 13.2 %copy-start.10 = (pred[32,64,128]{2,1,0:T(8,128)(4,1)S(1)}, pred[32,64,128]{2,1,0:T(8,128)(4,1)}, u32[]{:S(2)}) copy-start(pred[32,64,128]{2,1,0:T(8,128)(4,1)} %get-tuple-element.11) | copy-start | bytes 786436
  329.4 13.2 %copy-start.11 = (pred[32,64,128]{2,1,0:T(8,128)(4,1)S(1)}, pred[32,64,128]{2,1,0:T(8,128)(4,1)}, u32[]{:S(2)}) copy-start(pred[32,64,128]{2,1,0:T(8,128)(4,1)} %get-tuple-element.12) | copy-start | bytes 786436
  329.4 13.2 %copy-start.12 = (pred[32,64,128]{2,1,0:T(8,128)(4,1)S(1)}, pred[32,64,128]{2,1,0:T(8,128)(4,1)}, u32[]{:S(2)}) copy-start(pred[32,64,128]{2,1,0:T(8,128)(4,1)} %get-tuple-element.13) | copy-start | bytes 786436
  329.4 13.3 %copy-start.13 = (pred[32,64,128]{2,1,0:T(8,128)(4,1)S(1)}, pred[32,64,128]{2,1,0:T(8,128)(4,1)}, u32[]{:S(2)}) copy-start(pred[32,64,128]{2,1,0:T(8,128)(4,1)} %get-tuple-element.14) | copy-start | bytes 786436
  329.4 13.3 %copy-start.14 = (pred[32,64,128]{2,1,0:T(8,128)(4,1)S(1)}, pred[32,64,128]{2,1,0:T(8,128)(4,1)}, u32[]{:S(2)}) copy-start(pred[32,64,128]{2,1,0:T(8,128)(4,1)} %get-tuple-element.15) | copy-start | bytes 786436
  329.4 13.3 %copy-start.15 = (pred[32,64,128]{2,1,0:T(8,128)(4,1)S(1)}, pred[32,64,128]{2,1,0:T(8,128)(4,1)}, u32[]{:S(2)}) copy-start(pred[32,64,128]{2,1,0:T(8,128)(4,1)} %get-tuple-element.16) | copy-start | bytes 786436
  329.4 13.3 %copy-start.16 = (pred[32,64,128]{2,1,0:T(8,128)(4,1)S(1)}, pred[32,64,128]{2,1,0:T(8,128)(4,1)}, u32[]{:S(2)}) copy-start(pred[32,64,128]{2,1,0:T(8,128)(4,1)} %get-tuple-element.17) | copy-start | bytes 786436
  329.4 13.3 %copy-start.17 = (pred[32,64,128]{2,1,0:T(8,128)(4,1)S(1)}, pred[32,64,128]{2,1,0:T(8,128)(4,1)}, u32[]{:S(2)}) copy-start(pred[32,64,128]{2,1,0:T(8,128)(4,1)} %get-tuple-element.18) | copy-start | bytes 786436
  329.4 13.3 %copy-start.18 = (pred[32,64,128]{2,1,0:T(8,128)(4,1)S(1)}, pred[32,64,128]{2,1,0:T(8,128)(4,1)}, u32[]{:S(2)}) copy-start(pred[32,64,128]{2,1,0:T(8,128)(4,1)} %get-tuple-element.19) | copy-start | bytes 786436
  329.4 13.3 %copy-start.19 = (pred[32,64,128]{2,1,0:T(8,128)(4,1)S(1)}, pred[32,64,128]{2,1,0:T(8,128)(4,1)}, u32[]{:S(2)}) copy-start(pred[32,64,128]{2,1,0:T(8,128)(4,1)} %get-tuple-element.20) | copy-start | bytes 786436
  329.4 13.3 %copy-start.20 = (pred[32,64,128]{2,1,0:T(8,128)(4,1)S(1)}, pred[32,64,128]{2,1,0:T(8,128)(4,1)}, u32[]{:S(2)}) copy-start(pred[32,64,128]{2,1,0:T(8,128)(4,1)} %get-tuple-element.21) | copy-start | bytes 786436
  329.5 13.3 %copy-start.21 = (pred[32,64,128]{2,1,0:T(8,128)(4,1)S(1)}, pred[32,64,128]{2,1,0:T(8,128)(4,1)}, u32[]{:S(2)}) copy-start(pred[32,64,128]{2,1,0:T(8,128)(4,1)} %get-tuple-element.22) | copy-start | bytes 786436
  329.5 13.3 %copy-start.22 = (pred[32,64,128]{2,1,0:T(8,128)(4,1)S(1)}, pred[32,64,128]{2,1,0:T(8,128)(4,1)}, u32[]{:S(2)}) copy-start(pred[32,64,128]{2,1,0:T(8,128)(4,1)} %get-tuple-element.23) | copy-start | bytes 786436
  329.5 13.3 %copy-start.23 = (pred[32,64,128]{2,1,0:T(8,128)(4,1)S(1)}, pred[32,64,128]{2,1,0:T(8,128)(4,1)}, u32[]{:S(2)}) copy-start(pred[32,64,128]{2,1,0:T(8,128)(4,1)} %get-tuple-element.24) | copy-start | bytes 786436
  329.5 3.7 collective-permute-start.4
  331.1 6.4 %collective-permute-start.5 = (f32[3,1,64,128]{3,2,1,0:T(8,128)S(1)}, f32[3,1,64,128]{3,2,1,0:T(8,128)S(1)}, u32[]{:S(2)}, u32[]{:S(2)}) collective-permute-start(f32[3,1,64,128]{3,2,1,0:T(8,128)S(1)} %get-tuple-element.44), channel_id=1, source_target_pairs={{16,0},{32,16},{48,32},{64,48},{80,64},{96,80},{112,96},{17,1},{33... | collective-permute-start | bytes 294920 | tf_op jit(solution)/shard_map/ppermute | solution.py:21
  337.5 5.0 %collective-permute-start.6 = (f32[3,34,1,128]{3,2,1,0:T(1,128)S(1)}, f32[3,34,1,128]{3,2,1,0:T(1,128)S(1)}, u32[]{:S(2)}, u32[]{:S(2)}) collective-permute-start(f32[3,34,1,128]{3,2,1,0:T(1,128)S(1)} %get-tuple-element.43), channel_id=1, source_target_pairs={{0,1},{1,2},{2,3},{3,4},{4,5},{5,6},{6,7},{7,8},{8,9},{9,10},{10,1... | collective-permute-start | bytes 156680 | tf_op jit(solution)/shard_map/ppermute | solution.py:20
  340.2 27.5 %collective-permute-start.7 = (f32[3,34,1,128]{3,2,1,0:T(1,128)S(1)}, f32[3,34,1,128]{3,2,1,0:T(1,128)S(1)}, u32[]{:S(2)}, u32[]{:S(2)}) collective-permute-start(f32[3,34,1,128]{3,2,1,0:T(1,128)S(1)} %get-tuple-element.42), channel_id=1, source_target_pairs={{1,0},{2,1},{3,2},{4,3},{5,4},{6,5},{7,6},{8,7},{9,8},{10,9},{11,1... | collective-permute-start | bytes 156680 | tf_op jit(solution)/shard_map/ppermute | solution.py:21
  370.8 2.7 copy-start.4
where the time goes:
time: 432 us; the launch traced here: 424 us
  other arithmetic  168 us (39%)
  local copies, waits for them, and re-layouts  134 us (31%)
  starting transfers between devices  45.1 us (10%)
  waiting for transfers between devices  40.6 us (9%)
  blocking collectives  34.4 us (8%)
    scatter-add x1, other arithmetic, on_device(): stress.reshape(6, cells, depth).at[:, into_cells].add(moved[3:])  56.7 us
    scatter-add x1, other arithmetic, on_device(): velocity.reshape(3, cells, depth).at[:, into_cells].add(moved[:3])  54 us
    all_to_all x1, waiting for transfers between devices, on_device(): lax.all_to_all(outgoing, ('gx', 'gy'), split_axis=0, concat_axis=0, tiled...  36.2 us
    slice x1, local copies, waits for them, and re-layouts, ahead_y(): return padded[field, 1:-1, 2:] - middle[field]  34.6 us
    all_to_all x1, blocking collectives, on_device(): lax.all_to_all(outgoing_rows, ('gx', 'gy'), split_axis=0, concat_axis=0,...  34.4 us
    scatter x1, local copies, waits for them, and re-layouts, on_device(): jnp.zeros((devices * capacity, 9, depth), jnp.float32).at[send_slot]  26.5 us
    unnamed x7, other arithmetic  26.4 us
    unnamed x73, local copies, waits for them, and re-layouts  24.6 us
  transfers between devices with their start and end apart: 10, of which 3 were waited for; matrix products, arithmetic and copies ran while one was open for 40% of the time, Pallas kernels for 0%

commit v1 on v0

v1 whole, which is shorter than its diff:
```python
import functools

import jax
import jax.numpy as jnp
from jax import lax
from jax.experimental import pallas as pl
from jax.experimental.pallas import tpu as pltpu
from jax.sharding import PartitionSpec as P

PML = 8
STEP = 0.25
DAMP = 0.3
SLOTS = 4
GROUPS = 4
MESH = pl.DeviceIdType.MESH
F32 = jnp.float32
BF16 = jnp.bfloat16


def iota(shape, dim):
    return lax.broadcasted_iota(jnp.int32, shape, dim)


def split_in_two(values):
    high = values.astype(BF16)
    return high, (values - high.astype(F32)).astype(BF16)


def absorb(distance):
    ramp = jnp.maximum(0.0, (PML - distance) / PML)
    return 1.0 - DAMP * ramp * ramp


def z_before(field):
    return jnp.where(iota(field.shape, 1) == 0, 0.0, pltpu.roll(field, 1, 1))


def z_after(field):
    size = field.shape[1]
    return jnp.where(iota(field.shape, 1) == size - 1, 0.0, pltpu.roll(field, size - 1, 1))


def y_before(field):
    return jnp.where(iota(field.shape, 0) == 0, 0.0, pltpu.roll(field, 1, 0))


def y_after(field):
    size = field.shape[0]
    return jnp.where(iota(field.shape, 0) == size - 1, 0.0, pltpu.roll(field, size - 1, 0))


def column_of(row):
    size = row.shape[1]
    square = iota((size, size), 0) == iota((size, size), 1)
    return jnp.sum(jnp.where(square, row.astype(F32), 0.0), axis=1, keepdims=True)


def lookup(region, table_ref):
    values = [table_ref[i] for i in range(16)]
    for bit in range(4):
        mask = (region & (1 << bit)) != 0
        values = [jnp.where(mask, values[2 * i + 1], values[2 * i]) for i in range(len(values) // 2)]
    return values[0]


def peer(step, gx, gy):
    x = (gx + step) % 4
    y = (gy // 2 + step // 4 + step) % 4
    z = (gx // 4 + 2 * (gy // 8) + step // 16 + step) % 4
    core = (gy + step // 64 + step) % 2
    return (z % 2) * 4 + x, (z // 2) * 8 + y * 2 + core


def wave_kernel(
    target, cell, table_b, table_l, table_m, rows_in, velocity_in, stress_in, region_in,
    vel, st,
    rows, region, hb, hl, hm, parts, outgoing, arrived, group, y_send, x_halo, y_halo, v_send, vx_halo, vy_halo,
    load_sem, own_sem, send_sem, recv_sem, halo_send, halo_recv,
):
    gx, gy = lax.axis_index("gx"), lax.axis_index("gy")
    count_x, count_y = 8, 16
    devices = count_x * count_y
    me = gx * count_y + gy
    load_rows = pltpu.make_async_copy(rows_in, rows, load_sem.at[0])
    load_rows.start()
    load_region = pltpu.make_async_copy(region_in, region, load_sem.at[1])
    load_vel = pltpu.make_async_copy(velocity_in, vel, load_sem.at[2])
    load_st = pltpu.make_async_copy(stress_in, st, load_sem.at[3])
    load_region.start()
    load_vel.start()
    load_st.start()

    barrier = pltpu.get_barrier_semaphore()

    def greet(step, _):
        other = lax.rem(me + step, devices)
        pl.semaphore_signal(
            barrier, inc=1, device_id=(other // count_y, other % count_y), device_id_type=MESH
        )
        return 0

    lax.fori_loop(1, devices, greet, 0)

    target_row = target[...]
    count = target_row.shape[1]
    target_col = column_of(target_row).astype(jnp.int32)
    same = (target_col == target_row) & (iota((count, count), 0) < iota((count, count), 1))
    rank_row = jnp.sum(jnp.where(same, 1.0, 0.0), axis=0, keepdims=True)
    cell_row = cell[...].astype(F32)
    load_rows.wait()
    for f in range(9):
        high, low = split_in_two(rows[f])
        parts[0:count, f * 128 : (f + 1) * 128] = high
        parts[count : 2 * count, f * 128 : (f + 1) * 128] = low
    named = target_row == iota((devices, count), 0)
    cells_out = jnp.zeros((devices, 128), F32)
    lane_slot = iota((devices, 128), 1) // 32
    for k in range(SLOTS):
        mine = named & (rank_row == float(k))
        pick = jnp.where(mine, 1.0, 0.0).astype(BF16)
        pick = jnp.concatenate([pick, pick], axis=1)
        cell_col = jnp.sum(jnp.where(mine, cell_row, 0.0), axis=1, keepdims=True)
        cells_out = jnp.where(lane_slot == k, cell_col, cells_out)
        for first in range(0, 9, 2):
            width = min(2, 9 - first)
            packed = jnp.dot(
                pick, parts[:, first * 128 : (first + width) * 128], preferred_element_type=F32
            )
            for f in range(width):
                outgoing[(first + f) * SLOTS + k] = packed[:, f * 128 : (f + 1) * 128]
    outgoing[9 * SLOTS] = cells_out

    pl.semaphore_wait(barrier, devices - 1)
    per_group = devices // GROUPS

    def send(step, _):
        to_x, to_y = peer(step, gx, gy)
        pltpu.make_async_remote_copy(
            src_ref=outgoing.at[:, to_x * count_y + to_y, :],
            dst_ref=arrived.at[:, step, :],
            send_sem=send_sem,
            recv_sem=recv_sem.at[step // per_group],
            device_id=(to_x, to_y),
            device_id_type=MESH,
        ).start()
        return 0

    lax.fori_loop(1, devices, send, 0)
    own = pltpu.make_async_copy(outgoing.at[:, me, :], arrived.at[:, 0, :], own_sem)
    own.start()

    load_region.wait()

    def materials(x, _):
        here = region[x]
        hb[x] = STEP * lookup(here, table_b)
        hl[x] = STEP * lookup(here, table_l)
        hm[x] = STEP * lookup(here, table_m)
        return 0

    lax.fori_loop(0, 32, materials, 0)
    load_vel.wait()
    load_st.wait()
    own.wait()

    def add_group(g, first):
        for f in range(9):
            for k in range(SLOTS):
                high, low = split_in_two(arrived[f * SLOTS + k, pl.ds(first, 32), :])
                group[k * 32 : (k + 1) * 32, f * 128 : (f + 1) * 128] = high
                group[128 + k * 32 : 128 + (k + 1) * 32, f * 128 : (f + 1) * 128] = low
        names = arrived[9 * SLOTS, pl.ds(first, 32), :]
        mine = iota((32, 128), 1) % 32 == iota((32, 128), 0)
        names = jnp.sum(jnp.where(mine, names, 0.0), axis=0, keepdims=True).astype(jnp.int32)
        names = jnp.concatenate([names, names], axis=1)

        def add_block(block, _):
            pick = jnp.where(iota((256, 256), 0) + block * 256 == names, 1.0, 0.0).astype(BF16)
            for first in range(0, 9, 2):
                width = min(2, 9 - first)
                added = jnp.dot(
                    pick, group[:, first * 128 : (first + width) * 128], preferred_element_type=F32
                )
                for f in range(width):
                    piece = added[:, f * 128 : (f + 1) * 128].reshape(4, 64, 128)
                    if first + f < 3:
                        vel[first + f, pl.ds(block * 4, 4)] += piece
                    else:
                        st[first + f - 3, pl.ds(block * 4, 4)] += piece
            return 0

        lax.fori_loop(0, 8, add_block, 0)

    for g in range(GROUPS):
        low = 1 if g == 0 else 0
        landed = arrived.at[:, pl.ds(g * per_group + low, per_group - low), :]
        pltpu.make_async_remote_copy(
            src_ref=landed, dst_ref=landed, send_sem=send_sem, recv_sem=recv_sem.at[g],
            device_id=(gx, gy), device_id_type=MESH,
        ).wait_recv()
        add_group(g, g * per_group)

    x_after_dev = ((gx + 1) % count_x, gy)
    x_before_dev = ((gx + count_x - 1) % count_x, gy)
    y_after_dev = (gx, (gy + 1) % count_y)
    y_before_dev = (gx, (gy + count_y - 1) % count_y)
    has_x_before, has_x_after = gx > 0, gx < count_x - 1
    has_y_before, has_y_after = gy > 0, gy < count_y - 1

    def halo_copy(number, source, landing, device):
        return pltpu.make_async_remote_copy(
            src_ref=source, dst_ref=landing, send_sem=halo_send.at[number],
            recv_sem=halo_recv.at[number], device_id=device, device_id_type=MESH,
        )

    y_send[0] = st[3, :, 63:64, :]
    y_send[1] = st[5, :, 63:64, :]
    y_send[2] = st[1, :, 0:1, :]
    stress_copies = [
        halo_copy(0, st.at[0, 0], x_halo.at[0], x_before_dev),
        halo_copy(1, st.at[pl.ds(3, 2), 31], x_halo.at[pl.ds(1, 2)], x_after_dev),
        halo_copy(2, y_send.at[pl.ds(0, 2)], y_halo.at[pl.ds(0, 2)], y_after_dev),
        halo_copy(3, y_send.at[2], y_halo.at[2], y_before_dev),
    ]
    for copy in stress_copies:
        copy.start()

    def move_velocity(x, xx_after, xy_before, xz_before):
        xx, yy, zz, xy, xz, yz = [st[f, x] for f in range(6)]
        scaled = hb[x]
        vel[0, x] += scaled * ((xx_after - xx) + (xy - y_before(xy)) + (xz - z_before(xz)))
        vel[1, x] += scaled * ((xy - xy_before) + (y_after(yy) - yy) + (yz - z_before(yz)))
        vel[2, x] += scaled * ((xz - xz_before) + (yz - y_before(yz)) + (z_after(zz) - zz))

    def inner_velocity(x, _):
        move_velocity(x, st[0, x + 1], st[3, x - 1], st[4, x - 1])
        return 0

    lax.fori_loop(1, 31, inner_velocity, 0)
    for copy in stress_copies:
        copy.wait()
    move_velocity(
        0, st[0, 1], jnp.where(has_x_before, x_halo[1], 0.0), jnp.where(has_x_before, x_halo[2], 0.0)
    )
    move_velocity(31, jnp.where(has_x_after, x_halo[0], 0.0), st[3, 30], st[4, 30])
    top, bottom = hb[:, 0:1, :], hb[:, 63:64, :]
    vel[0, :, 0:1, :] -= top * jnp.where(has_y_before, y_halo[0], 0.0)
    vel[2, :, 0:1, :] -= top * jnp.where(has_y_before, y_halo[1], 0.0)
    vel[1, :, 63:64, :] += bottom * jnp.where(has_y_after, y_halo[2], 0.0)

    v_send[0] = vel[1, :, 63:64, :]
    v_send[1] = vel[0, :, 0:1, :]
    v_send[2] = vel[2, :, 0:1, :]
    velocity_copies = [
        halo_copy(4, vel.at[0, 31], vx_halo.at[0], x_after_dev),
        halo_copy(5, vel.at[pl.ds(1, 2), 0], vx_halo.at[pl.ds(1, 2)], x_before_dev),
        halo_copy(6, v_send.at[0], vy_halo.at[0], y_after_dev),
        halo_copy(7, v_send.at[pl.ds(1, 2)], vy_halo.at[pl.ds(1, 2)], y_before_dev),
    ]
    for copy in velocity_copies:
        copy.start()

    def move_stress(x, vx_before, vy_after, vz_after):
        vx, vy, vz = [vel[c, x] for c in range(3)]
        first, shear = hl[x], hm[x]
        strain_x, strain_y, strain_z = vx - vx_before, vy - y_before(vy), vz - z_before(vz)
        spread = first * (strain_x + strain_y + strain_z)
        twice = 2.0 * shear
        st[0, x] += spread + twice * strain_x
        st[1, x] += spread + twice * strain_y
        st[2, x] += spread + twice * strain_z
        st[3, x] += shear * ((vy_after - vy) + (y_after(vx) - vx))
        st[4, x] += shear * ((vz_after - vz) + (z_after(vx) - vx))
        st[5, x] += shear * ((y_after(vz) - vz) + (z_after(vy) - vy))

    def inner_stress(x, _):
        move_stress(x, vel[0, x - 1], vel[1, x + 1], vel[2, x + 1])
        return 0

    lax.fori_loop(1, 31, inner_stress, 0)
    for copy in velocity_copies:
        copy.wait()
    move_stress(0, jnp.where(has_x_before, vx_halo[0], 0.0), vel[1, 1], vel[2, 1])
    move_stress(
        31, vel[0, 30], jnp.where(has_x_after, vx_halo[1], 0.0), jnp.where(has_x_after, vx_halo[2], 0.0)
    )
    vy_edge = jnp.where(has_y_before, vy_halo[0], 0.0)
    first, shear = hl[:, 0:1, :], hm[:, 0:1, :]
    st[0, :, 0:1, :] -= first * vy_edge
    st[1, :, 0:1, :] -= (first + 2.0 * shear) * vy_edge
    st[2, :, 0:1, :] -= first * vy_edge
    shear = hm[:, 63:64, :]
    st[3, :, 63:64, :] += shear * jnp.where(has_y_after, vy_halo[1], 0.0)
    st[5, :, 63:64, :] += shear * jnp.where(has_y_after, vy_halo[2], 0.0)

    sent = outgoing.at[:, pl.ds(0, devices - 1), :]
    pltpu.make_async_remote_copy(
        src_ref=sent, dst_ref=sent, send_sem=send_sem, recv_sem=recv_sem.at[0],
        device_id=(gx, gy), device_id_type=MESH,
    ).wait_send()


def finish_kernel(
    pile_cell, vel, st, pile_pier, owner, vel_out, st_out, partial, damped_v, damped_s, traction, sems
):
    gx, gy = lax.axis_index("gx"), lax.axis_index("gy")
    y_index = gy * 64 + iota((64, 128), 0)
    along_y = absorb(jnp.minimum(y_index, 1023 - y_index).astype(F32))
    along_z = absorb((127 - iota((64, 128), 1)).astype(F32))
    plane = along_y * along_z

    def damp(step, _):
        for i in range(4):
            x = step * 4 + i
            x_index = gx * 32 + x
            far = jnp.broadcast_to(jnp.minimum(x_index, 255 - x_index), (64, 128)).astype(F32)
            factor = absorb(far) * plane
            for c in range(3):
                damped_v[c, x] = vel[c, x] * factor
            for f in range(6):
                damped_s[f, x] = st[f, x] * factor
        planes = pl.ds(step * 4, 4)
        pltpu.make_async_copy(damped_v.at[:, planes], vel_out.at[:, planes], sems.at[0]).start()
        pltpu.make_async_copy(damped_s.at[:, planes], st_out.at[:, planes], sems.at[1]).start()
        return 0

    lax.fori_loop(0, 8, damp, 0)

    def fetch(p, _):
        at = pile_cell[p]
        x, y = at // 64, at % 64
        for c, f in enumerate((4, 5, 2)):
            traction[c, pl.ds(p, 1), :] = damped_s[f, x, pl.ds(y, 1), :]
        return 0

    lax.fori_loop(0, 256, fetch, 0, unroll=8)
    pier_row = pile_pier[...]
    owner_col = column_of(owner[...])
    named = pier_row == iota((128, 256), 0)
    slot_row = jnp.sum(jnp.where(named, owner_col, 0.0), axis=0, keepdims=True).astype(jnp.int32)
    pick = jnp.where(slot_row == iota((128, 256), 0), 1.0, 0.0).astype(BF16)
    pick = jnp.concatenate([pick, pick], axis=1)
    response = jnp.concatenate([jnp.tanh(traction[c]) for c in range(3)], axis=1)
    high, low = split_in_two(response)
    both = jnp.concatenate([high, low], axis=0)
    partial[...] = jnp.dot(pick, both, preferred_element_type=F32)
    pltpu.make_async_copy(damped_v, vel_out, sems.at[0]).wait()
    pltpu.make_async_copy(damped_s, st_out, sems.at[1]).wait()


def pier_kernel(partial, force, first, second, rows, send_one, recv_one, send_two, recv_two):
    gx, gy = lax.axis_index("gx"), lax.axis_index("gy")
    barrier = pltpu.get_barrier_semaphore()
    for k in range(1, 8):
        pl.semaphore_signal(barrier, inc=1, device_id=((gx + k) % 8, gy), device_id_type=MESH)
    for k in range(1, 16):
        pl.semaphore_signal(barrier, inc=1, device_id=(gx, (gy + k) % 16), device_id_type=MESH)
    pl.semaphore_wait(barrier, 22)

    copies = []
    for k in range(1, 8):
        to = (gx + k) % 8
        copies.append(
            pltpu.make_async_remote_copy(
                src_ref=partial.at[pl.ds(pl.multiple_of(to * 16, 16), 16)],
                dst_ref=first.at[k - 1],
                send_sem=send_one.at[k - 1],
                recv_sem=recv_one.at[k - 1],
                device_id=(to, gy),
                device_id_type=MESH,
            )
        )
    for copy in copies:
        copy.start()
    total = partial[pl.ds(pl.multiple_of(gx * 16, 16), 16), :]
    for k, copy in enumerate(copies):
        copy.wait_recv()
        total = total + first[k]
    for j in range(16):
        rows[j] = total[j : j + 1, :]
    more = []
    for k in range(1, 16):
        to = (gy + k) % 16
        more.append(
            pltpu.make_async_remote_copy(
                src_ref=rows.at[to],
                dst_ref=second.at[k - 1],
                send_sem=send_two.at[k - 1],
                recv_sem=recv_two.at[k - 1],
                device_id=(gx, to),
                device_id_type=MESH,
            )
        )
    for copy in more:
        copy.start()
    result = rows[gy]
    for k, copy in enumerate(more):
        copy.wait_recv()
        result = result + second[k]
    force[...] = result * (1.0 / 256.0) ** 0.5
    for copy in copies + more:
        copy.wait_send()


def on_device(
    velocity,
    stress,
    region_id,
    buoyancy,
    lame_lambda,
    shear_mu,
    shell_rows,
    shell_target,
    shell_cell,
    pile_pier,
    pile_cell,
    pier_owner,
):
    vmem = pl.BlockSpec(memory_space=pltpu.VMEM)
    smem = pl.BlockSpec(memory_space=pltpu.SMEM)
    anywhere = pl.BlockSpec(memory_space=pl.ANY)
    dma = pltpu.SemaphoreType.DMA
    vel, st = pl.pallas_call(
        wave_kernel,
        out_shape=(pltpu.VMEM((3, 32, 64, 128), F32), pltpu.VMEM((6, 32, 64, 128), F32)),
        in_specs=[vmem, vmem, smem, smem, smem, anywhere, anywhere, anywhere, anywhere],
        out_specs=(vmem, vmem),
        scratch_shapes=[
            pltpu.VMEM((9, 256, 128), F32),
            pltpu.VMEM((32, 64, 128), jnp.int32),
            pltpu.VMEM((32, 64, 128), F32),
            pltpu.VMEM((32, 64, 128), F32),
            pltpu.VMEM((32, 64, 128), F32),
            pltpu.VMEM((512, 1152), BF16),
            pltpu.VMEM((37, 128, 128), F32),
            pltpu.VMEM((37, 128, 128), F32),
            pltpu.VMEM((256, 1152), BF16),
            pltpu.VMEM((3, 32, 1, 128), F32),
            pltpu.VMEM((3, 64, 128), F32),
            pltpu.VMEM((3, 32, 1, 128), F32),
            pltpu.VMEM((3, 32, 1, 128), F32),
            pltpu.VMEM((3, 64, 128), F32),
            pltpu.VMEM((3, 32, 1, 128), F32),
            dma((4,)),
            dma,
            dma,
            dma((GROUPS,)),
            dma((8,)),
            dma((8,)),
        ],
        compiler_params=pltpu.CompilerParams(
            collective_id=0, has_side_effects=True, vmem_limit_bytes=40 << 20
        ),
    )(
        shell_target.reshape(1, 256),
        shell_cell.reshape(1, 256),
        buoyancy,
        lame_lambda,
        shear_mu,
        jnp.transpose(shell_rows, (1, 0, 2)),
        velocity,
        stress,
        region_id,
    )
    velocity_out, stress_out, partial = pl.pallas_call(
        finish_kernel,
        out_shape=(
            jax.ShapeDtypeStruct((3, 32, 64, 128), F32),
            jax.ShapeDtypeStruct((6, 32, 64, 128), F32),
            jax.ShapeDtypeStruct((128, 384), F32),
        ),
        in_specs=[smem, vmem, vmem, vmem, vmem],
        out_specs=(anywhere, anywhere, vmem),
        scratch_shapes=[
            pltpu.VMEM((3, 32, 64, 128), F32),
            pltpu.VMEM((6, 32, 64, 128), F32),
            pltpu.VMEM((3, 256, 128), F32),
            dma((2,)),
        ],
        compiler_params=pltpu.CompilerParams(vmem_limit_bytes=40 << 20),
    )(
        pile_cell.reshape(256),
        vel,
        st,
        pile_pier.reshape(1, 256),
        pier_owner.reshape(1, 128),
    )
    pier_force = pl.pallas_call(
        pier_kernel,
        out_shape=jax.ShapeDtypeStruct((1, 384), F32),
        in_specs=[vmem],
        out_specs=vmem,
        scratch_shapes=[
            pltpu.VMEM((7, 16, 384), F32),
            pltpu.VMEM((15, 1, 384), F32),
            pltpu.VMEM((16, 1, 384), F32),
            dma((7,)),
            dma((7,)),
            dma((15,)),
            dma((15,)),
        ],
        compiler_params=pltpu.CompilerParams(collective_id=1, has_side_effects=True),
    )(partial)
    return velocity_out, stress_out, pier_force


def solution(mesh):
    return jax.shard_map(
        on_device,
        mesh=mesh,
        in_specs=(
            P(None, "gx", "gy", None),
            P(None, "gx", "gy", None),
            P("gx", "gy", None),
            P(),
            P(),
            P(),
            P(("gx", "gy"), None, None),
            P(("gx", "gy"), None),
            P(("gx", "gy"), None),
            P(("gx", "gy"), None),
            P(("gx", "gy"), None),
            P(),
        ),
        out_specs=(P(None, "gx", "gy", None), P(None, "gx", "gy", None), P(("gx", "gy"), None)),
        check_vma=False,
    )
```

time: 432 us -> 82.9 us (0.19); the launches traced: 424 us -> 82.6 us
  other arithmetic: 168 us -> 0 us
  local copies, waits for them, and re-layouts: 134 us -> 7.71 us
  Pallas kernels: 0 us -> 74.1 us
  starting transfers between devices: 45.1 us -> 0 us
  waiting for transfers between devices: 40.6 us -> 0 us
  blocking collectives: 34.4 us -> 0 us
    scatter-add x2 -> x0, other arithmetic: 111 us -> none  [the longest x1 56.7 us: on_device(): stress.reshape(6, cells, depth).at[:, into_cells].add(moved[3:])]
    pallas_call x0 -> x3, Pallas kernels: none -> 74.1 us  [the longest x1 53.2 us: on_device(): pl.pallas_call(wave_kernel, out_shape=(pltpu.VMEM((3, 32, 64, 128), F32),...]
    slice x15 -> x0, local copies, waits for them, and re-layouts: 51.8 us -> none  [the longest x1 34.6 us: ahead_y(): return padded[field, 1:-1, 2:] - middle[field]]
    all_to_all x2 -> x0, waiting for transfers between devices: 36.2 us -> none  [the longest x1 36.2 us: on_device(): lax.all_to_all(outgoing, ('gx', 'gy'), split_axis=0, concat_axis=0, tiled...]
    scatter x3 -> x0, local copies, waits for them, and re-layouts: 34.9 us -> none  [the longest x1 26.5 us: on_device(): jnp.zeros((devices * capacity, 9, depth), jnp.float32).at[send_slot]]
    all_to_all x1 -> x0, blocking collectives: 34.4 us -> none  [on_device(): lax.all_to_all(outgoing_rows, ('gx', 'gy'), split_axis=0, concat_axis=0,...]
    unnamed x7 -> x0, other arithmetic: 26.4 us -> none
    ppermute x8 -> x0, starting transfers between devices: 22.8 us -> none  [the longest x4 15.8 us: with_halo(): after = lax.ppermute(leading, axis, down)]
  transfers between devices with their start and end apart: 10 -> 0, of which waited for: 3 -> 0; matrix products, arithmetic and copies ran while one was open for 40% -> 0% of each run, Pallas kernels for 0% -> 0%
where the time goes in v1:
time: 82.9 us; the launch traced here: 82.6 us
  Pallas kernels  74.1 us (89%)
  local copies, waits for them, and re-layouts  7.71 us (9%)
    pallas_call x1, Pallas kernels, on_device(): pl.pallas_call(wave_kernel, out_shape=(pltpu.VMEM((3, 32, 64, 128), F32),...  53.2 us
    pallas_call x1, Pallas kernels, on_device(): pl.pallas_call(pier_kernel, out_shape=jax.ShapeDtypeStruct((1, 384), F32)...  16.6 us
    unnamed x23, local copies, waits for them, and re-layouts  7.71 us
    pallas_call x1, Pallas kernels, on_device(): pl.pallas_call(finish_kernel, out_shape=(jax.ShapeDtypeStruct((3, 32, 64,...  4.28 us

profile of v1, /device:TPU:1, one launch (start us, length us, event | category | flops | bytes accessed | tf_op | source)
XLA Modules:
  0.0 82.6 jit_solution(12311367214702563270)
XLA Ops:
  0.6 0.0 copy-start
  0.6 1.3 %copy-done = f32[256,9,128]{2,0,1:T(8,128)S(1)} copy-done((f32[256,9,128]{2,0,1:T(8,128)S(1)}, f32[256,9,128]{2,0,1:T(8,128)}, u32[]{:S(2)}) %copy-start) | copy-done | bytes 1179672
  1.9 0.0 copy-start.1
  1.9 1.2 %copy-done.1 = s32[32,64,128]{2,1,0:T(8,128)S(1)} copy-done((s32[32,64,128]{2,1,0:T(8,128)S(1)}, s32[32,64,128]{2,1,0:T(8,128)}, u32[]{:S(2)}) %copy-start.1) | copy-done | bytes 1048600
  3.1 0.0 copy-start.3
  3.1 0.7 copy-done.3
  3.8 0.0 copy-start.4
  3.8 0.7 copy-done.4
  4.5 0.0 copy-start.7
  4.5 0.7 copy-done.7
  5.1 0.0 copy-start.8
  5.1 0.7 copy-done.8
  5.8 0.0 copy-start.9
  5.8 0.7 copy-done.9
  6.5 0.0 copy-start.5
  6.5 0.0 copy-start.6
  6.5 0.0 copy-start.10
  6.5 53.2 %shard_map.139 = (f32[3,32,64,128]{3,2,1,0:T(8,128)S(1)}, f32[6,32,64,128]{3,2,1,0:T(8,128)S(1)}) custom-call(s32[1,256]{1,0:T(1,128)S(1)} %bitcast.7, s32[1,256]{1,0:T(1,128)S(1)} %bitcast.8, f32[16]{0:T(128)S(1)} %copy-done.7, f32[16]{0:T(128)S(1)} %copy-done.8, f32[16]{0:T(128)S(1)} %copy-done.9, f32[9,256,128]{2,1,0:T(8,128)S(1)} %bitcast.6, ...), custom_call_target="tpu_custom_call" | custom-call | tf_op jit(solution)/shard_map/pallas_call | solution.py:423
  59.7 0.0 copy-done.5
  59.7 0.0 copy-done.6
  59.7 0.0 copy-done.10
  59.7 4.3 %shard_map.140 = (f32[3,32,64,128]{3,2,1,0:T(8,128)}, f32[6,32,64,128]{3,2,1,0:T(8,128)}, f32[128,384]{1,0:T(8,128)S(1)}) custom-call(s32[256]{0:T(256)S(1)} %bitcast.9, f32[3,32,64,128]{3,2,1,0:T(8,128)S(1)} %get-tuple-element.8.vel, f32[6,32,64,128]{3,2,1,0:T(8,128)S(1)} %get-tuple-element.9.st, s32[1,256]{1,0:T(1,128)S(1)} %bitcast.10, s32[1,128]{1,0:T(1,128)S(1)} %bitcast.11), custom_call_target="tpu_custom_call" | custom-call | tf_op jit(solution)/shard_map/pallas_call | solution.py:465
  64.0 0.0 copy-start.2
  64.0 0.7 copy-done.2
  64.7 16.6 %shard_map.141 = f32[1,384]{1,0:T(1,128)} custom-call(f32[128,384]{1,0:T(8,128)} %copy-done.2), custom_call_target="tpu_custom_call" | custom-call | tf_op jit(solution)/shard_map/pallas_call | solution.py:488
  81.3 1.2 %copy.16 = f32[1,384]{1,0:T(1,128)} copy(f32[1,384]{1,0:T(1,128)} %shard_map.141) | data formatting | bytes 3072
Async XLA Ops:
  0.6 1.3 %copy-start = (f32[256,9,128]{2,0,1:T(8,128)S(1)}, f32[256,9,128]{2,0,1:T(8,128)}, u32[]{:S(2)}) copy-start(f32[256,9,128]{2,0,1:T(8,128)} %param.18) | copy-start | bytes 3538948
  1.9 1.2 %copy-start.1 = (s32[32,64,128]{2,1,0:T(8,128)S(1)}, s32[32,64,128]{2,1,0:T(8,128)}, u32[]{:S(2)}) copy-start(s32[32,64,128]{2,1,0:T(8,128)} %region_in.1) | copy-start | bytes 3145732
  3.1 0.7 copy-start.3
  3.8 0.7 copy-start.4
  4.5 0.7 copy-start.7
  5.1 0.7 copy-start.8
  5.8 0.7 copy-start.9
  6.5 53.2 %copy-start.5 = (s32[256,1]{0,1:T(1,128)S(1)}, s32[256,1]{0,1:T(1,128)}, u32[]{:S(2)}) copy-start(s32[256,1]{0,1:T(1,128)} %param.22) | copy-start | bytes 3076
  6.5 53.2 %copy-start.6 = (s32[256,1]{0,1:T(1,128)S(1)}, s32[256,1]{0,1:T(1,128)}, u32[]{:S(2)}) copy-start(s32[256,1]{0,1:T(1,128)} %param.21) | copy-start | bytes 3076
  6.5 53.3 %copy-start.10 = (s32[128]{0:T(128)S(1)}, s32[128]{0:T(128)}, u32[]{:S(2)}) copy-start(s32[128]{0:T(128)} %param.23) | copy-start | bytes 1540
  64.0 0.7 copy-start.2

commit v2 on v1

v2 whole, which is shorter than its diff:
```python
import functools

import jax
import jax.numpy as jnp
from jax import lax
from jax.experimental import pallas as pl
from jax.experimental.pallas import tpu as pltpu
from jax.sharding import PartitionSpec as P

PML = 8
STEP = 0.25
DAMP = 0.3
SLOTS = 4
GROUPS = 4
UNROLL = 4
MESH = pl.DeviceIdType.MESH
LOGICAL = pl.DeviceIdType.LOGICAL
F32 = jnp.float32
BF16 = jnp.bfloat16


def iota(shape, dim):
    return lax.broadcasted_iota(jnp.int32, shape, dim)


def split_in_two(values):
    high = values.astype(BF16)
    return high, (values - high.astype(F32)).astype(BF16)


def absorb(distance):
    ramp = jnp.maximum(0.0, (PML - distance) / PML)
    return 1.0 - DAMP * ramp * ramp


def z_before(field):
    return jnp.where(iota(field.shape, 1) == 0, 0.0, pltpu.roll(field, 1, 1))


def z_after(field):
    size = field.shape[1]
    return jnp.where(iota(field.shape, 1) == size - 1, 0.0, pltpu.roll(field, size - 1, 1))


def y_before(field):
    return jnp.where(iota(field.shape, 0) == 0, 0.0, pltpu.roll(field, 1, 0))


def y_after(field):
    size = field.shape[0]
    return jnp.where(iota(field.shape, 0) == size - 1, 0.0, pltpu.roll(field, size - 1, 0))


def column_of(row):
    size = row.shape[1]
    square = iota((size, size), 0) == iota((size, size), 1)
    return jnp.sum(jnp.where(square, row.astype(F32), 0.0), axis=1, keepdims=True)


def lookup(region, table_ref):
    values = [table_ref[i] for i in range(16)]
    for bit in range(4):
        mask = (region & (1 << bit)) != 0
        values = [jnp.where(mask, values[2 * i + 1], values[2 * i]) for i in range(len(values) // 2)]
    return values[0]


def peer(step, gx, gy):
    x = lax.rem(gx + step, 4)
    y = lax.rem(lax.div(gy, 2) + lax.div(step, 4) + step, 4)
    z = lax.rem(lax.div(gx, 4) + 2 * lax.div(gy, 8) + lax.div(step, 16) + step, 4)
    core = lax.rem(gy + lax.div(step, 64) + step, 2)
    return lax.rem(z, 2) * 64 + x * 16 + lax.div(z, 2) * 8 + y * 2 + core


def wave_kernel(
    target_in, cell_in, table_b_in, table_l_in, table_m_in, rows_in, velocity_in, stress_in, region_in,
    pile_cell_in, pile_pier_in, owner_in,
    vel, st, force,
    target, cell, table_b, table_l, table_m, rows, region, hb, hl, hm,
    pile_at, pile_cell, pile_pier, owner, traction, response, sums, sums_in,
    parts, outgoing, arrived, group, x_send, y_send, x_halo, y_halo, v_send, vx_halo, vy_halo,
    load_sem, own_sem, send_sem, recv_sem, halo_send, halo_recv, sums_send, sums_recv,
):
    gx, gy = lax.axis_index("gx"), lax.axis_index("gy")
    count_x, count_y = 8, 16
    devices = count_x * count_y
    me = gx * count_y + gy
    loads = [
        pltpu.make_async_copy(source, landing, load_sem.at[i])
        for i, (source, landing) in enumerate((
            (target_in, target), (cell_in, cell), (rows_in, rows),
            (table_b_in, table_b), (table_l_in, table_l), (table_m_in, table_m), (region_in, region),
            (velocity_in, vel), (stress_in, st), (pile_cell_in, pile_at), (pile_cell_in, pile_cell),
            (pile_pier_in, pile_pier), (owner_in, owner),
        ))
    ]
    for load in loads:
        load.start()

    barrier = pltpu.get_barrier_semaphore()

    def greet(step, _):
        pl.semaphore_signal(
            barrier, inc=1, device_id=lax.rem(me + step, devices), device_id_type=LOGICAL
        )
        return 0

    lax.fori_loop(1, devices, greet, 0, unroll=8)
    for load in loads[:3]:
        load.wait()

    target_row = target[...]
    count = target_row.shape[1]
    target_col = column_of(target_row).astype(jnp.int32)
    same = (target_col == target_row) & (iota((count, count), 0) < iota((count, count), 1))
    rank_row = jnp.sum(jnp.where(same, 1.0, 0.0), axis=0, keepdims=True)
    cell_row = cell[...].astype(F32)
    for f in range(9):
        high, low = split_in_two(rows[f])
        parts[0:count, f * 128 : (f + 1) * 128] = high
        parts[count : 2 * count, f * 128 : (f + 1) * 128] = low
    named = target_row == iota((devices, count), 0)
    cells_out = jnp.zeros((devices, 128), F32)
    lane_slot = iota((devices, 128), 1) // 32
    for k in range(SLOTS):
        mine = named & (rank_row == float(k))
        pick = jnp.where(mine, 1.0, 0.0).astype(BF16)
        pick = jnp.concatenate([pick, pick], axis=1)
        cell_col = jnp.sum(jnp.where(mine, cell_row, 0.0), axis=1, keepdims=True)
        cells_out = jnp.where(lane_slot == k, cell_col, cells_out)
        for first in range(0, 9, 2):
            width = min(2, 9 - first)
            packed = jnp.dot(
                pick, parts[:, first * 128 : (first + width) * 128], preferred_element_type=F32
            )
            for f in range(width):
                outgoing[(first + f) * SLOTS + k] = packed[:, f * 128 : (f + 1) * 128]
    outgoing[9 * SLOTS] = cells_out

    pl.semaphore_wait(barrier, devices - 1)
    per_group = devices // GROUPS

    def send(step, _):
        to = peer(step, gx, gy)
        pltpu.make_async_remote_copy(
            src_ref=outgoing.at[:, to, :],
            dst_ref=arrived.at[:, step, :],
            send_sem=send_sem,
            recv_sem=recv_sem.at[lax.div(step, per_group)],
            device_id=to,
            device_id_type=LOGICAL,
        ).start()
        return 0

    lax.fori_loop(1, devices, send, 0, unroll=8)
    own = pltpu.make_async_copy(outgoing.at[:, me, :], arrived.at[:, 0, :], own_sem)
    own.start()

    for load in loads[3:]:
        load.wait()

    def materials(x, _):
        here = region[x]
        hb[x] = STEP * lookup(here, table_b)
        hl[x] = STEP * lookup(here, table_l)
        hm[x] = STEP * lookup(here, table_m)
        return 0

    lax.fori_loop(0, 32, materials, 0)
    at = column_of(pile_cell[...].reshape(1, 256)).astype(jnp.int32)
    pile_x, pile_y = gx * 32 + at // 64, gy * 64 + at % 64
    plane = absorb(jnp.minimum(pile_x, 255 - pile_x).astype(F32))
    plane = plane * absorb(jnp.minimum(pile_y, 1023 - pile_y).astype(F32))
    pile_factor = plane * absorb((127 - iota((256, 128), 1)).astype(F32))
    owner_col = column_of(owner[...])
    named = pile_pier[...] == iota((devices, 256), 0)
    slot_row = jnp.sum(jnp.where(named, owner_col, 0.0), axis=0, keepdims=True).astype(jnp.int32)
    owned = jnp.where(slot_row == iota((devices, 256), 0), 1.0, 0.0).astype(BF16)
    owned = jnp.concatenate([owned, owned], axis=1)
    own.wait()

    def gather_group(first):
        for f in range(9):
            for k in range(SLOTS):
                high, low = split_in_two(arrived[f * SLOTS + k, pl.ds(first, 32), :])
                group[k * 32 : (k + 1) * 32, f * 128 : (f + 1) * 128] = high
                group[128 + k * 32 : 128 + (k + 1) * 32, f * 128 : (f + 1) * 128] = low
        names = arrived[9 * SLOTS, pl.ds(first, 32), :]
        mine = iota((32, 128), 1) % 32 == iota((32, 128), 0)
        names = jnp.sum(jnp.where(mine, names, 0.0), axis=0, keepdims=True).astype(jnp.int32)
        return jnp.concatenate([names, names], axis=1)

    def add_group(names):
        def add_block(block, _):
            pick = jnp.where(iota((256, 256), 0) + block * 256 == names, 1.0, 0.0).astype(BF16)
            for first in range(0, 9, 2):
                width = min(2, 9 - first)
                added = jnp.dot(
                    pick, group[:, first * 128 : (first + width) * 128], preferred_element_type=F32
                )
                for f in range(width):
                    piece = added[:, f * 128 : (f + 1) * 128].reshape(4, 64, 128)
                    if first + f < 3:
                        vel[first + f, pl.ds(block * 4, 4)] += piece
                    else:
                        st[first + f - 3, pl.ds(block * 4, 4)] += piece
            return 0

        lax.fori_loop(0, 8, add_block, 0, unroll=UNROLL)

    for g in range(GROUPS):
        low = 1 if g == 0 else 0
        landed = arrived.at[:, pl.ds(g * per_group + low, per_group - low), :]
        pltpu.make_async_remote_copy(
            src_ref=landed, dst_ref=landed, send_sem=send_sem, recv_sem=recv_sem.at[g],
            device_id=(gx, gy), device_id_type=MESH,
        ).wait_recv()
        names = gather_group(g * per_group)
        if g < GROUPS - 1:
            add_group(names)

    x_after_dev = ((gx + 1) % count_x, gy)
    x_before_dev = ((gx + count_x - 1) % count_x, gy)
    y_after_dev = (gx, (gy + 1) % count_y)
    y_before_dev = (gx, (gy + count_y - 1) % count_y)
    has_x_before, has_x_after = gx > 0, gx < count_x - 1
    has_y_before, has_y_after = gy > 0, gy < count_y - 1

    def halo_copy(number, source, landing, device):
        return pltpu.make_async_remote_copy(
            src_ref=source, dst_ref=landing, send_sem=halo_send.at[number],
            recv_sem=halo_recv.at[number], device_id=device, device_id_type=MESH,
        )

    row = iota((192, 1), 0)
    column = jnp.where(row < 64, row, row + 31 * 64 - 64)
    column = jnp.where(row >= 128, (row - 128) * 64 + 63, column)
    column = jnp.where(row >= 160, (row - 160) * 64, column)
    pick = jnp.where(column == names, 1.0, 0.0).astype(BF16)
    edge = jnp.dot(pick, group[:, 384:1152], preferred_element_type=F32)
    x_send[0] = st[0, 0] + edge[0:64, 0:128]
    x_send[1] = st[3, 31] + edge[64:128, 384:512]
    x_send[2] = st[4, 31] + edge[64:128, 512:640]
    y_send[0] = st[3, :, 63:64, :] + edge[128:160, 384:512].reshape(32, 1, 128)
    y_send[1] = st[5, :, 63:64, :] + edge[128:160, 640:768].reshape(32, 1, 128)
    y_send[2] = st[1, :, 0:1, :] + edge[160:192, 128:256].reshape(32, 1, 128)
    stress_copies = [
        halo_copy(0, x_send.at[0], x_halo.at[0], x_before_dev),
        halo_copy(1, x_send.at[pl.ds(1, 2)], x_halo.at[pl.ds(1, 2)], x_after_dev),
        halo_copy(2, y_send.at[pl.ds(0, 2)], y_halo.at[pl.ds(0, 2)], y_after_dev),
        halo_copy(3, y_send.at[2], y_halo.at[2], y_before_dev),
    ]
    for copy in stress_copies:
        copy.start()
    add_group(names)

    def move_velocity(x, xx_after, xy_before, xz_before):
        xx, yy, zz, xy, xz, yz = [st[f, x] for f in range(6)]
        scaled = hb[x]
        vel[0, x] += scaled * ((xx_after - xx) + (xy - y_before(xy)) + (xz - z_before(xz)))
        vel[1, x] += scaled * ((xy - xy_before) + (y_after(yy) - yy) + (yz - z_before(yz)))
        vel[2, x] += scaled * ((xz - xz_before) + (yz - y_before(yz)) + (z_after(zz) - zz))

    def inner_velocity(x, _):
        move_velocity(x, st[0, x + 1], st[3, x - 1], st[4, x - 1])
        return 0

    lax.fori_loop(1, 31, inner_velocity, 0, unroll=2)
    for copy in stress_copies:
        copy.wait()
    move_velocity(
        0, st[0, 1], jnp.where(has_x_before, x_halo[1], 0.0), jnp.where(has_x_before, x_halo[2], 0.0)
    )
    move_velocity(31, jnp.where(has_x_after, x_halo[0], 0.0), st[3, 30], st[4, 30])
    top, bottom = hb[:, 0:1, :], hb[:, 63:64, :]
    vel[0, :, 0:1, :] -= top * jnp.where(has_y_before, y_halo[0], 0.0)
    vel[2, :, 0:1, :] -= top * jnp.where(has_y_before, y_halo[1], 0.0)
    vel[1, :, 63:64, :] += bottom * jnp.where(has_y_after, y_halo[2], 0.0)

    v_send[0] = vel[1, :, 63:64, :]
    v_send[1] = vel[0, :, 0:1, :]
    v_send[2] = vel[2, :, 0:1, :]
    velocity_copies = [
        halo_copy(4, vel.at[0, 31], vx_halo.at[0], x_after_dev),
        halo_copy(5, vel.at[pl.ds(1, 2), 0], vx_halo.at[pl.ds(1, 2)], x_before_dev),
        halo_copy(6, v_send.at[0], vy_halo.at[0], y_after_dev),
        halo_copy(7, v_send.at[pl.ds(1, 2)], vy_halo.at[pl.ds(1, 2)], y_before_dev),
    ]
    for copy in velocity_copies:
        copy.start()

    def move_pulled(x, vx_before, vz_after):
        vx, vy, vz = [vel[c, x] for c in range(3)]
        first, shear = hl[x], hm[x]
        strain_z = vz - z_before(vz)
        spread = first * ((vx - vx_before) + (vy - y_before(vy)) + strain_z)
        st[2, x] += spread + 2.0 * shear * strain_z
        st[4, x] += shear * ((vz_after - vz) + (z_after(vx) - vx))
        st[5, x] += shear * ((y_after(vz) - vz) + (z_after(vy) - vy))

    def inner_pulled(x, _):
        move_pulled(x, vel[0, x - 1], vel[2, x + 1])
        return 0

    lax.fori_loop(1, 31, inner_pulled, 0, unroll=2)
    for copy in velocity_copies:
        copy.wait()
    vx_edge = jnp.where(has_x_before, vx_halo[0], 0.0)
    move_pulled(0, vx_edge, vel[2, 1])
    move_pulled(31, vel[0, 30], jnp.where(has_x_after, vx_halo[2], 0.0))
    st[2, :, 0:1, :] -= hl[:, 0:1, :] * jnp.where(has_y_before, vy_halo[0], 0.0)
    st[5, :, 63:64, :] += hm[:, 63:64, :] * jnp.where(has_y_after, vy_halo[2], 0.0)

    def fetch(p, _):
        at = pile_at[p]
        x, y = lax.div(at, 64), lax.rem(at, 64)
        for c, f in enumerate((4, 5, 2)):
            traction[c, pl.ds(p, 1), :] = st[f, x, pl.ds(y, 1), :]
        return 0

    lax.fori_loop(0, 256, fetch, 0, unroll=8)
    for c in range(3):
        high, low = split_in_two(jnp.tanh(traction[c] * pile_factor))
        response[0:256, c * 128 : (c + 1) * 128] = high
        response[256:512, c * 128 : (c + 1) * 128] = low
    total = jnp.dot(owned, response[...], preferred_element_type=F32)
    for c in range(3):
        sums[c] = total[:, c * 128 : (c + 1) * 128]

    def send_sum(step, _):
        to = lax.rem(me + step, devices)
        pltpu.make_async_remote_copy(
            src_ref=sums.at[:, to, :], dst_ref=sums_in.at[:, step, :],
            send_sem=sums_send, recv_sem=sums_recv, device_id=to, device_id_type=LOGICAL,
        ).start()
        return 0

    lax.fori_loop(1, devices, send_sum, 0, unroll=8)
    def move_rest(x, vx_before, vy_after):
        vx, vy, vz = [vel[c, x] for c in range(3)]
        first, shear = hl[x], hm[x]
        row = iota(vx.shape, 0)
        vy_before = jnp.where(row == 0, jnp.where(has_y_before, vy_halo[0, x], 0.0), pltpu.roll(vy, 1, 0))
        vx_after = jnp.where(row == 63, jnp.where(has_y_after, vy_halo[1, x], 0.0), pltpu.roll(vx, 63, 0))
        strain_x, strain_y, strain_z = vx - vx_before, vy - vy_before, vz - z_before(vz)
        spread = first * (strain_x + strain_y + strain_z)
        st[0, x] += spread + 2.0 * shear * strain_x
        st[1, x] += spread + 2.0 * shear * strain_y
        st[3, x] += shear * ((vy_after - vy) + (vx_after - vx))

    def inner_rest(x, _):
        move_rest(x, vel[0, x - 1], vel[1, x + 1])
        return 0

    move_rest(0, vx_edge, vel[1, 1])
    lax.fori_loop(1, 31, inner_rest, 0, unroll=2)
    move_rest(31, vel[0, 30], jnp.where(has_x_after, vx_halo[1], 0.0))

    y_index = gy * 64 + iota((64, 128), 0)
    along_y = absorb(jnp.minimum(y_index, 1023 - y_index).astype(F32))
    factor_yz = along_y * absorb((127 - iota((64, 128), 1)).astype(F32))

    def damp(x, _):
        x_index = gx * 32 + x
        far = jnp.broadcast_to(jnp.minimum(x_index, 255 - x_index), (64, 128)).astype(F32)
        factor = absorb(far) * factor_yz
        for c in range(3):
            vel[c, x] *= factor
        for f in range(6):
            st[f, x] *= factor
        return 0

    lax.fori_loop(0, 32, damp, 0)
    sent = outgoing.at[:, pl.ds(0, devices - 1), :]
    pltpu.make_async_remote_copy(
        src_ref=sent, dst_ref=sent, send_sem=send_sem, recv_sem=recv_sem.at[0],
        device_id=(gx, gy), device_id_type=MESH,
    ).wait_send()
    sums_in[:, 0:1, :] = sums[:, pl.ds(me, 1), :]
    landed = sums_in.at[:, pl.ds(1, devices - 1), :]
    pltpu.make_async_remote_copy(
        src_ref=landed, dst_ref=landed, send_sem=sums_send, recv_sem=sums_recv,
        device_id=(gx, gy), device_id_type=MESH,
    ).wait()
    for c in range(3):
        here = jnp.sum(sums_in[c], axis=0, keepdims=True)
        force[:, c * 128 : (c + 1) * 128] = here * (1.0 / 256.0) ** 0.5


def finish_kernel(vel, st, force, vel_out, st_out, force_out, sems):
    copies = [
        pltpu.make_async_copy(vel, vel_out, sems.at[0]),
        pltpu.make_async_copy(st.at[pl.ds(0, 3)], st_out.at[pl.ds(0, 3)], sems.at[1]),
        pltpu.make_async_copy(st.at[pl.ds(3, 3)], st_out.at[pl.ds(3, 3)], sems.at[2]),
    ]
    for copy in copies:
        copy.start()
    force_out[...] = force[...]
    for copy in copies:
        copy.wait()


def on_device(
    velocity,
    stress,
    region_id,
    buoyancy,
    lame_lambda,
    shear_mu,
    shell_rows,
    shell_target,
    shell_cell,
    pile_pier,
    pile_cell,
    pier_owner,
):
    vmem = pl.BlockSpec(memory_space=pltpu.VMEM)
    anywhere = pl.BlockSpec(memory_space=pl.ANY)
    in_hbm = pl.BlockSpec(memory_space=pltpu.HBM)
    dma = pltpu.SemaphoreType.DMA
    operands = (
        shell_target.reshape(1, 256),
        shell_cell.reshape(1, 256),
        buoyancy,
        lame_lambda,
        shear_mu,
        jnp.transpose(shell_rows, (1, 0, 2)),
        velocity,
        stress,
        region_id,
        pile_cell.reshape(256),
        pile_pier.reshape(1, 256),
        pier_owner.reshape(1, 128),
    )
    operands = [pltpu.with_memory_space_constraint(x, pltpu.HBM) for x in operands]
    fields = pltpu.VMEM((32, 64, 128), F32)
    edge_row = pltpu.VMEM((3, 32, 1, 128), F32)
    edge_plane = pltpu.VMEM((3, 64, 128), F32)
    table = pltpu.SMEM((16,), F32)
    vel, st, force = pl.pallas_call(
        wave_kernel,
        out_shape=(
            pltpu.VMEM((3, 32, 64, 128), F32), pltpu.VMEM((6, 32, 64, 128), F32), pltpu.VMEM((1, 384), F32)
        ),
        in_specs=[in_hbm] * len(operands),
        out_specs=(vmem, vmem, vmem),
        scratch_shapes=[
            pltpu.VMEM((1, 256), jnp.int32),
            pltpu.VMEM((1, 256), jnp.int32),
            table,
            table,
            table,
            pltpu.VMEM((9, 256, 128), F32),
            pltpu.VMEM((32, 64, 128), jnp.int32),
            fields,
            fields,
            fields,
            pltpu.SMEM((256,), jnp.int32),
            pltpu.VMEM((256,), jnp.int32),
            pltpu.VMEM((1, 256), jnp.int32),
            pltpu.VMEM((1, 128), jnp.int32),
            pltpu.VMEM((3, 256, 128), F32),
            pltpu.VMEM((512, 384), BF16),
            pltpu.VMEM((3, 128, 128), F32),
            pltpu.VMEM((3, 128, 128), F32),
            pltpu.VMEM((512, 1152), BF16),
            pltpu.VMEM((37, 128, 128), F32),
            pltpu.VMEM((37, 128, 128), F32),
            pltpu.VMEM((256, 1152), BF16),
            edge_plane,
            edge_row,
            edge_plane,
            edge_row,
            edge_row,
            edge_plane,
            edge_row,
            dma((13,)),
            dma,
            dma,
            dma((GROUPS,)),
            dma((8,)),
            dma((8,)),
            dma,
            dma,
        ],
        compiler_params=pltpu.CompilerParams(
            collective_id=0, has_side_effects=True, vmem_limit_bytes=40 << 20
        ),
    )(*operands)
    return pl.pallas_call(
        finish_kernel,
        out_shape=(
            jax.ShapeDtypeStruct((3, 32, 64, 128), F32),
            jax.ShapeDtypeStruct((6, 32, 64, 128), F32),
            jax.ShapeDtypeStruct((1, 384), F32),
        ),
        in_specs=[vmem, vmem, vmem],
        out_specs=(anywhere, anywhere, vmem),
        scratch_shapes=[
            dma((3,)),
        ],
        compiler_params=pltpu.CompilerParams(vmem_limit_bytes=40 << 20),
    )(vel, st, force)


def solution(mesh):
    return jax.shard_map(
        on_device,
        mesh=mesh,
        in_specs=(
            P(None, "gx", "gy", None),
            P(None, "gx", "gy", None),
            P("gx", "gy", None),
            P(),
            P(),
            P(),
            P(("gx", "gy"), None, None),
            P(("gx", "gy"), None),
            P(("gx", "gy"), None),
            P(("gx", "gy"), None),
            P(("gx", "gy"), None),
            P(),
        ),
        out_specs=(P(None, "gx", "gy", None), P(None, "gx", "gy", None), P(("gx", "gy"), None)),
        check_vma=False,
    )
```

time: 82.9 us -> 64.3 us (0.78)
  Pallas kernels: 74.1 us -> 63.6 us
  local copies, waits for them, and re-layouts: 7.71 us -> 0 us
    pallas_call x1 -> x0, Pallas kernels: 16.6 us -> none  [on_device(): pl.pallas_call(pier_kernel, out_shape=jax.ShapeDtypeStruct((1, 384), F32)...]
    unnamed x23 -> x0, local copies, waits for them, and re-layouts: 7.71 us -> none
    pallas_call x1, Pallas kernels: 53.2 us -> 59.3 us  [on_device(): pl.pallas_call(wave_kernel, out_shape=(pltpu.VMEM((3, 32, 64, 128), F32),...]
where the time goes in v2:
time: 64.3 us; the launch traced here: 64.2 us
  Pallas kernels  63.6 us (99%)
    pallas_call x1, Pallas kernels, on_device(): pl.pallas_call(wave_kernel, out_shape=(pltpu.VMEM((3, 32, 64, 128), F32),...  59.3 us
    pallas_call x1, Pallas kernels, on_device(): pl.pallas_call(finish_kernel, out_shape=(jax.ShapeDtypeStruct((3, 32, 64,...  4.32 us

profile of v2, /device:TPU:1, one launch (start us, length us, event | category | flops | bytes accessed | tf_op | source)
XLA Modules:
  0.0 64.2 jit_solution(13979955875664399903)
XLA Ops:
  0.6 59.3 %shard_map.139 = (f32[3,32,64,128]{3,2,1,0:T(8,128)S(1)}, f32[6,32,64,128]{3,2,1,0:T(8,128)S(1)}, f32[1,384]{1,0:T(1,128)S(1)}) custom-call(s32[1,256]{1,0:T(1,128)} %bitcast.7, s32[1,256]{1,0:T(1,128)} %bitcast.8, f32[16]{0:T(128)} %table_b_in.1, f32[16]{0:T(128)} %table_l_in.1, f32[16]{0:T(128)} %table_m_in.1, f32[9,256,128]{2,1,0:T(8,128)} %bitcast.6, ...), custom_call_target="tpu_custom_call" | custom-call | tf_op jit(solution)/shard_map/pallas_call | solution.py:441
  59.9 4.3 %shard_map.140 = (f32[3,32,64,128]{3,2,1,0:T(8,128)}, f32[6,32,64,128]{3,2,1,0:T(8,128)}, f32[1,384]{1,0:T(1,128)}) custom-call(f32[3,32,64,128]{3,2,1,0:T(8,128)S(1)} %get-tuple-element.6.vel, f32[6,32,64,128]{3,2,1,0:T(8,128)S(1)} %get-tuple-element.7.st, f32[1,384]{1,0:T(1,128)S(1)} %get-tuple-element.8.force), custom_call_target="tpu_custom_call" | custom-call | tf_op jit(solution)/shard_map/pallas_call | solution.py:491

commit v3 on v2

--- a/solution.py
+++ b/solution.py
@@ -80,7 +80,7 @@
     target, cell, table_b, table_l, table_m, rows, region, hb, hl, hm,
     pile_at, pile_cell, pile_pier, owner, traction, response, sums, sums_in,
     parts, outgoing, arrived, group, x_send, y_send, x_halo, y_halo, v_send, vx_halo, vy_halo,
-    load_sem, own_sem, send_sem, recv_sem, halo_send, halo_recv, sums_send, sums_recv,
+    load_sem, own_sem, send_sem, recv_sem, halo_send, halo_recv, sums_send, sums_recv, on_edge, change,
 ):
     gx, gy = lax.axis_index("gx"), lax.axis_index("gy")
     count_x, count_y = 8, 16
@@ -178,6 +178,13 @@
     slot_row = jnp.sum(jnp.where(named, owner_col, 0.0), axis=0, keepdims=True).astype(jnp.int32)
     owned = jnp.where(slot_row == iota((devices, 256), 0), 1.0, 0.0).astype(BF16)
     owned = jnp.concatenate([owned, owned], axis=1)
+    lane = iota((1, 256), 1)
+    edge_of = jnp.where(lane < 64, lane, lane + 31 * 64 - 64)
+    edge_of = jnp.where(lane >= 128, (lane - 128) * 64, edge_of)
+    edge_of = jnp.where(lane >= 160, (lane - 160) * 64 + 63, edge_of)
+    edge_of = jnp.where(lane >= 192, -1, edge_of)
+    on_edge[...] = jnp.where(at == edge_of, 1.0, 0.0).astype(BF16)
+    change[...] = jnp.zeros(change.shape, BF16)
     own.wait()
 
     def gather_group(first):
@@ -303,14 +310,10 @@
         move_pulled(x, vel[0, x - 1], vel[2, x + 1])
         return 0
 
+    nothing = jnp.zeros((64, 128), F32)
+    move_pulled(0, nothing, vel[2, 1])
     lax.fori_loop(1, 31, inner_pulled, 0, unroll=2)
-    for copy in velocity_copies:
-        copy.wait()
-    vx_edge = jnp.where(has_x_before, vx_halo[0], 0.0)
-    move_pulled(0, vx_edge, vel[2, 1])
-    move_pulled(31, vel[0, 30], jnp.where(has_x_after, vx_halo[2], 0.0))
-    st[2, :, 0:1, :] -= hl[:, 0:1, :] * jnp.where(has_y_before, vy_halo[0], 0.0)
-    st[5, :, 63:64, :] += hm[:, 63:64, :] * jnp.where(has_y_after, vy_halo[2], 0.0)
+    move_pulled(31, vel[0, 30], nothing)
 
     def fetch(p, _):
         at = pile_at[p]
@@ -320,8 +323,26 @@
         return 0
 
     lax.fori_loop(0, 256, fetch, 0, unroll=8)
+    for copy in velocity_copies:
+        copy.wait()
+    vx_edge = jnp.where(has_x_before, vx_halo[0], 0.0)
+    vy_edge = jnp.where(has_y_before, vy_halo[0], 0.0)
+    vz_edge = jnp.where(has_y_after, vy_halo[2], 0.0)
+    zz_x = -hl[0] * vx_edge
+    xz_x = hm[31] * jnp.where(has_x_after, vx_halo[2], 0.0)
+    zz_y = -hl[:, 0:1, :] * vy_edge
+    yz_y = hm[:, 63:64, :] * vz_edge
+    for first, count, c, part in (
+        (0, 64, 2, zz_x), (64, 64, 0, xz_x), (128, 32, 2, zz_y.reshape(32, 128)), (160, 32, 1, yz_y.reshape(32, 128))
+    ):
+        high, low = split_in_two(part)
+        change[first : first + count, c * 128 : (c + 1) * 128] = high
+        change[256 + first : 256 + first + count, c * 128 : (c + 1) * 128] = low
+    pick = jnp.concatenate([on_edge[...], on_edge[...]], axis=1)
+    changes = jnp.dot(pick, change[...], preferred_element_type=F32)
     for c in range(3):
-        high, low = split_in_two(jnp.tanh(traction[c] * pile_factor))
+        pulled = traction[c] + changes[:, c * 128 : (c + 1) * 128]
+        high, low = split_in_two(jnp.tanh(pulled * pile_factor))
         response[0:256, c * 128 : (c + 1) * 128] = high
         response[256:512, c * 128 : (c + 1) * 128] = low
     total = jnp.dot(owned, response[...], preferred_element_type=F32)
@@ -337,6 +358,11 @@
         return 0
 
     lax.fori_loop(1, devices, send_sum, 0, unroll=8)
+    st[2, 0] += zz_x
+    st[4, 31] += xz_x
+    st[2, :, 0:1, :] += zz_y
+    st[5, :, 63:64, :] += yz_y
+
     def move_rest(x, vx_before, vy_after):
         vx, vy, vz = [vel[c, x] for c in range(3)]
         first, shear = hl[x], hm[x]
@@ -483,6 +509,8 @@
             dma((8,)),
             dma,
             dma,
+            pltpu.VMEM((256, 256), BF16),
+            pltpu.VMEM((512, 384), BF16),
         ],
         compiler_params=pltpu.CompilerParams(
             collective_id=0, has_side_effects=True, vmem_limit_bytes=40 << 20

time: 64.3 us -> 63.9 us (level)
  no operation moved by 1% of the time
where the time goes in v3:
time: 63.9 us; the launch traced here: 63.8 us
  Pallas kernels  63.1 us (99%)
  between operations  0.64 us (1%)
    pallas_call x1, Pallas kernels, on_device(): pl.pallas_call(wave_kernel, out_shape=(pltpu.VMEM((3, 32, 64, 128), F32),...  58.8 us
    pallas_call x1, Pallas kernels, on_device(): pl.pallas_call(finish_kernel, out_shape=(jax.ShapeDtypeStruct((3, 32, 64,...  4.32 us

profile of v3, /device:TPU:1, one launch (start us, length us, event | category | flops | bytes accessed | tf_op | source)
XLA Modules:
  0.0 63.8 jit_solution(18030907567572287733)
XLA Ops:
  0.6 58.8 %shard_map.139 = (f32[3,32,64,128]{3,2,1,0:T(8,128)S(1)}, f32[6,32,64,128]{3,2,1,0:T(8,128)S(1)}, f32[1,384]{1,0:T(1,128)S(1)}) custom-call(s32[1,256]{1,0:T(1,128)} %bitcast.7, s32[1,256]{1,0:T(1,128)} %bitcast.8, f32[16]{0:T(128)} %table_b_in.1, f32[16]{0:T(128)} %table_l_in.1, f32[16]{0:T(128)} %table_m_in.1, f32[9,256,128]{2,1,0:T(8,128)} %bitcast.6, ...), custom_call_target="tpu_custom_call" | custom-call | tf_op jit(solution)/shard_map/pallas_call | solution.py:467
  59.4 4.3 %shard_map.140 = (f32[3,32,64,128]{3,2,1,0:T(8,128)}, f32[6,32,64,128]{3,2,1,0:T(8,128)}, f32[1,384]{1,0:T(1,128)}) custom-call(f32[3,32,64,128]{3,2,1,0:T(8,128)S(1)} %get-tuple-element.6.vel, f32[6,32,64,128]{3,2,1,0:T(8,128)S(1)} %get-tuple-element.7.st, f32[1,384]{1,0:T(1,128)S(1)} %get-tuple-element.8.force), custom_call_target="tpu_custom_call" | custom-call | tf_op jit(solution)/shard_map/pallas_call | solution.py:519

commit v4 on v3

--- a/solution.py
+++ b/solution.py
@@ -240,6 +240,18 @@
             recv_sem=halo_recv.at[number], device_id=device, device_id_type=MESH,
         )
 
+    x_up, x_down = (has_x_after, has_x_before), (has_x_before, has_x_after)
+    y_up, y_down = (has_y_after, has_y_before), (has_y_before, has_y_after)
+
+    def start_halo(copies, ways):
+        for copy, (sends, _) in zip(copies, ways):
+            pl.when(sends)(copy.start)
+
+    def wait_halo(copies, ways):
+        for copy, (sends, receives) in zip(copies, ways):
+            pl.when(sends)(copy.wait_send)
+            pl.when(receives)(copy.wait_recv)
+
     row = iota((192, 1), 0)
     column = jnp.where(row < 64, row, row + 31 * 64 - 64)
     column = jnp.where(row >= 128, (row - 128) * 64 + 63, column)
@@ -258,8 +270,8 @@
         halo_copy(2, y_send.at[pl.ds(0, 2)], y_halo.at[pl.ds(0, 2)], y_after_dev),
         halo_copy(3, y_send.at[2], y_halo.at[2], y_before_dev),
     ]
-    for copy in stress_copies:
-        copy.start()
+    stress_ways = (x_down, x_up, y_up, y_down)
+    start_halo(stress_copies, stress_ways)
     add_group(names)
 
     def move_velocity(x, xx_after, xy_before, xz_before):
@@ -274,8 +286,7 @@
         return 0
 
     lax.fori_loop(1, 31, inner_velocity, 0, unroll=2)
-    for copy in stress_copies:
-        copy.wait()
+    wait_halo(stress_copies, stress_ways)
     move_velocity(
         0, st[0, 1], jnp.where(has_x_before, x_halo[1], 0.0), jnp.where(has_x_before, x_halo[2], 0.0)
     )
@@ -294,8 +305,8 @@
         halo_copy(6, v_send.at[0], vy_halo.at[0], y_after_dev),
         halo_copy(7, v_send.at[pl.ds(1, 2)], vy_halo.at[pl.ds(1, 2)], y_before_dev),
     ]
-    for copy in velocity_copies:
-        copy.start()
+    velocity_ways = (x_up, x_down, y_up, y_down)
+    start_halo(velocity_copies, velocity_ways)
 
     def move_pulled(x, vx_before, vz_after):
         vx, vy, vz = [vel[c, x] for c in range(3)]
@@ -323,8 +334,7 @@
         return 0
 
     lax.fori_loop(0, 256, fetch, 0, unroll=8)
-    for copy in velocity_copies:
-        copy.wait()
+    wait_halo(velocity_copies, velocity_ways)
     vx_edge = jnp.where(has_x_before, vx_halo[0], 0.0)
     vy_edge = jnp.where(has_y_before, vy_halo[0], 0.0)
     vz_edge = jnp.where(has_y_after, vy_halo[2], 0.0)

time: 63.9 us -> 63.8 us (level)
  no operation moved by 1% of the time
where the time goes in v4:
time: 63.8 us; the launch traced here: 63.7 us
  Pallas kernels  63.1 us (99%)
  between operations  0.64 us (1%)
    pallas_call x1, Pallas kernels, on_device(): pl.pallas_call(wave_kernel, out_shape=(pltpu.VMEM((3, 32, 64, 128), F32),...  58.7 us
    pallas_call x1, Pallas kernels, on_device(): pl.pallas_call(finish_kernel, out_shape=(jax.ShapeDtypeStruct((3, 32, 64,...  4.32 us

profile of v4, /device:TPU:1, one launch (start us, length us, event | category | flops | bytes accessed | tf_op | source)
XLA Modules:
  0.0 63.7 jit_solution(9420922371796923350)
XLA Ops:
  0.6 58.7 %shard_map.139 = (f32[3,32,64,128]{3,2,1,0:T(8,128)S(1)}, f32[6,32,64,128]{3,2,1,0:T(8,128)S(1)}, f32[1,384]{1,0:T(1,128)S(1)}) custom-call(s32[1,256]{1,0:T(1,128)} %bitcast.7, s32[1,256]{1,0:T(1,128)} %bitcast.8, f32[16]{0:T(128)} %table_b_in.1, f32[16]{0:T(128)} %table_l_in.1, f32[16]{0:T(128)} %table_m_in.1, f32[9,256,128]{2,1,0:T(8,128)} %bitcast.6, ...), custom_call_target="tpu_custom_call" | custom-call | tf_op jit(solution)/shard_map/pallas_call | solution.py:477
  59.4 4.3 %shard_map.140 = (f32[3,32,64,128]{3,2,1,0:T(8,128)}, f32[6,32,64,128]{3,2,1,0:T(8,128)}, f32[1,384]{1,0:T(1,128)}) custom-call(f32[3,32,64,128]{3,2,1,0:T(8,128)S(1)} %get-tuple-element.6.vel, f32[6,32,64,128]{3,2,1,0:T(8,128)S(1)} %get-tuple-element.7.st, f32[1,384]{1,0:T(1,128)S(1)} %get-tuple-element.8.force), custom_call_target="tpu_custom_call" | custom-call | tf_op jit(solution)/shard_map/pallas_call | solution.py:529
